TPU v7x, 32 devices: a whole 2x2x4 slice. The times are simulated.
32 devices in a mesh: dp: 8 (over y, x, core), tensor: 4 (over z).
Axes of the slice: x: 2, y: 2, z: 4, core: 2. Of those that a mesh axis runs over, the one named last changes fastest.
Arguments:
- tokens: bfloat16 [1152, 8, 1024], P('tensor', 'dp'), may hold values from -6 to 6
- segment_ids: int32 [8, 1152], P('dp'), may hold values from 0 to 2, as said below
- norm1_gain: float32 [1024], replicated, may hold values from 0.5 to 1.5
- w_query: bfloat16 [1024, 1024], P(None, 'tensor'), may hold values from -0.046875 to 0.046875
- w_key: bfloat16 [1024, 1024], P(None, 'tensor'), may hold values from -0.1875 to 0.1875
- w_value: bfloat16 [1024, 1024], P(None, 'tensor'), may hold values from -0.1875 to 0.1875
- w_out: bfloat16 [1024, 1024], P('tensor'), may hold values from -0.375 to 0.375
- rel_bias: float32 [32, 16], P(None, 'tensor'), may hold values from -4 to 4
- norm2_gain: float32 [1024], replicated, may hold values from 0.5 to 1.5
- gate_weight_matrix: bfloat16 [1024, 2816], P(None, 'tensor'), may hold values from -0.1875 to 0.1875
- upward_weight: bfloat16 [1024, 2816], P(None, 'tensor'), may hold values from -0.1875 to 0.1875
- downward_weight: bfloat16 [2816, 1024], P('tensor'), may hold values from -0.15625 to 0.15625
- cotangent: bfloat16 [1152, 8, 1024], P('tensor', 'dp'), may hold values from -6 to 6
Outputs:
- out_tokens: bfloat16 [1152, 8, 1024], P('tensor', 'dp')
- grad_tokens: bfloat16 [1152, 8, 1024], P('tensor', 'dp')
- grad_norm1: float32 [1024], replicated
- grad_query: float32 [1024, 1024], P(None, 'tensor')
- grad_key: float32 [1024, 1024], P(None, 'tensor')
- grad_value: float32 [1024, 1024], P(None, 'tensor')
- grad_out: float32 [1024, 1024], P('tensor')
- grad_bias: float32 [32, 16], P(None, 'tensor')
- grad_norm2: float32 [1024], replicated
- gate_weight_gradient: float32 [1024, 2816], P(None, 'tensor')
- upward_weight_gradient: float32 [1024, 2816], P(None, 'tensor')
- downward_weight_gradient: float32 [2816, 1024], P('tensor')
- rms_stats: float32 [3], replicated
Inputs may be any that keep to these rules, and one draw needn't show every extreme that they name: `segment_ids`: in each row the ids are either all 0 (one example) or position // (384) (three examples of equal length); both kinds occur in every draw.
All inputs are finite; a program needn't handle non-finite values.
Results may differ from a plain program's by a relative error of at most 0.02.
Values may be sent and summed in bfloat16 or wider, within the bound.
No kernel may reach another device: no remote copies, remote signals or barrier semaphores. Data moves between devices by JAX's collectives and lax.ppermute only.
A program may use at most 192 MiB of HBM per device.

v0:
```python
import functools
from jax.sharding import PartitionSpec as P
import jax
import jax.numpy as jnp
from jax import lax
from jax.experimental import pallas as pl
from jax.experimental.pallas import tpu as pltpu

EPSILON = 1e-06
THRESHOLDS = (12, 16, 23, 32, 46, 64, 91)
TILE = 128
SEG = 384
NT = (((1,), (1,)), ((), ()))
TN = (((0,), (0,)), ((), ()))
F32 = jnp.float32
BF16 = jnp.bfloat16


def bucket_of(offset):
    distance = jnp.abs(offset)
    far_bucket = 8 + sum(((distance >= threshold).astype(jnp.int32) for threshold in THRESHOLDS))
    return jnp.where(distance < 8, distance, far_bucket) + 16 * (offset > 0).astype(jnp.int32)


def tile_bucket(delta, key_axis):
    keys = lax.broadcasted_iota(jnp.int32, (TILE, TILE), key_axis)
    queries = lax.broadcasted_iota(jnp.int32, (TILE, TILE), 1 - key_axis)
    return bucket_of(TILE * delta + keys - queries)


def bias_tiles_kernel(bias_ref, rows_ref, cols_ref):
    buckets, heads = bias_ref.shape
    for out_ref, key_axis in ((rows_ref, 1), (cols_ref, 0)):
        for delta in (-1, 0, 1):
            bucket = tile_bucket(delta, key_axis)
            tiles = [jnp.zeros((TILE, TILE), F32) for _ in range(heads)]
            for b in range(buckets):
                hit = bucket == b
                tiles = [jnp.where(hit, bias_ref[b, h], t) for h, t in enumerate(tiles)]
            for h in range(heads):
                out_ref[h, delta + 1] = tiles[h]


def bias_tiles(rel_bias):
    heads = rel_bias.shape[1]
    shape = jax.ShapeDtypeStruct((heads, 3, TILE, TILE), F32)
    return pl.pallas_call(
        bias_tiles_kernel,
        out_shape=(shape, shape),
        in_specs=[pl.BlockSpec(memory_space=pltpu.SMEM)],
        out_specs=(pl.BlockSpec(memory_space=pltpu.VMEM),) * 2,
        name="bias_tiles",
    )(rel_bias)


def bias_grad_kernel(near_ref, far_ref, out_ref):
    heads = near_ref.shape[0]
    row = lax.broadcasted_iota(jnp.int32, (32, TILE), 0)
    lane = lax.broadcasted_iota(jnp.int32, (32, TILE), 1)
    bucket = [tile_bucket(delta, 0) for delta in (-1, 0, 1)]
    total = jnp.zeros((32, TILE), F32)
    for h in range(heads):
        near = [near_ref[h, d] for d in range(3)]
        for b in range(32):
            deltas = (0, 1) if b < 16 else (1, 2)
            part = sum(jnp.where(bucket[d] == b, near[d], 0.0) for d in deltas)
            part = jnp.sum(part.reshape(16, 8, TILE), axis=0)
            if b == 15:
                part = part + far_ref[h, 0]
            if b == 31:
                part = part + far_ref[h, 1]
            line = jnp.sum(part, axis=0, keepdims=True)
            total = jnp.where((row == b) & (lane == h), jnp.sum(line, axis=1, keepdims=True), total)
    out_ref[...] = total


def bias_grad(near, far):
    return pl.pallas_call(
        bias_grad_kernel,
        out_shape=jax.ShapeDtypeStruct((32, TILE), F32),
        name="bias_grad",
    )(near, far)


def attn_fwd_kernel(seg_ref, bias_ref, q_ref, k_ref, v_ref, tile_ref, o_ref, lse_ref, s_ref, p_ref, l_ref):
    length, width = q_ref.shape
    heads = width // 64
    n_tiles = length // TILE
    lane = lax.broadcasted_iota(jnp.int32, (1, width), 1)
    one_example = seg_ref[0, length - 1] == seg_ref[0, 0]

    def blocks(h, mask, spans):
        for lo, hi in spans:
            qh = jnp.where(mask, q_ref[lo:hi], jnp.zeros((), BF16))
            s_ref[lo:hi, lo:hi] = lax.dot_general(qh, k_ref[lo:hi], NT, preferred_element_type=F32)
            below = bias_ref[15, h]
            above = bias_ref[31, h]
            for i in range(lo // TILE, hi // TILE):
                rows = slice(i * TILE, (i + 1) * TILE)
                near = range(max(lo // TILE, i - 1), min(hi // TILE, i + 2))
                parts = {j: s_ref[rows, j * TILE : (j + 1) * TILE] for j in range(lo // TILE, hi // TILE)}
                top = None
                for j in near:
                    parts[j] = parts[j] + tile_ref[h, j - i + 1]
                    top = parts[j] if top is None else jnp.maximum(top, parts[j])
                for side, constant in ((range(lo // TILE, near[0]), below), (range(near[-1] + 1, hi // TILE), above)):
                    if len(side):
                        far = functools.reduce(jnp.maximum, [parts[j] for j in side])
                        top = jnp.maximum(top, far + constant)
                top = jnp.max(top, axis=1, keepdims=True)
                total = None
                for j, part in parts.items():
                    if j < near[0]:
                        shift = top - below
                    elif j > near[-1]:
                        shift = top - above
                    else:
                        shift = top
                    e = jnp.exp(part - shift)
                    total = e if total is None else total + e
                    p_ref[rows, j * TILE : (j + 1) * TILE] = e.astype(BF16)
                total = jnp.sum(total, axis=1, keepdims=True)
                l_ref[rows] = jnp.broadcast_to(1.0 / total, (TILE, TILE))
                lse = jnp.broadcast_to(top + jnp.log(total), (TILE, TILE))
                lse_ref[h, :, rows] = jnp.transpose(lse)[:8]
            oh = lax.dot_general(p_ref[lo:hi, lo:hi], v_ref[lo:hi], (((1,), (0,)), ((), ())), preferred_element_type=F32)
            scale = l_ref[lo:hi, :1]
            o_ref[lo:hi] = jnp.where(mask, (oh * scale).astype(BF16), o_ref[lo:hi])

    @pl.loop(0, heads)
    def _(h):
        mask = (lane // 64) == h

        @pl.when(one_example)
        def _():
            blocks(h, mask, ((0, length),))

        @pl.when(jnp.logical_not(one_example))
        def _():
            blocks(h, mask, tuple((lo, lo + SEG) for lo in range(0, length, SEG)))


def attn_fwd(seg, bias, q, k, v, tiles):
    length, width = q.shape
    heads = width // 64
    vmem = pl.BlockSpec(memory_space=pltpu.VMEM)
    smem = pl.BlockSpec(memory_space=pltpu.SMEM)
    return pl.pallas_call(
        attn_fwd_kernel,
        out_shape=(
            jax.ShapeDtypeStruct((length, width), BF16),
            jax.ShapeDtypeStruct((heads, 8, length), F32),
        ),
        in_specs=[smem, smem, vmem, vmem, vmem, vmem],
        out_specs=(vmem, vmem),
        scratch_shapes=[
            pltpu.VMEM((length, length), F32),
            pltpu.VMEM((length, length), BF16),
            pltpu.VMEM((length, TILE), F32),
        ],
        compiler_params=pltpu.CompilerParams(vmem_limit_bytes=40 << 20),
        cost_estimate=pl.CostEstimate(flops=20_000_000_000, bytes_accessed=4_000_000, transcendentals=5_000_000),
        name="attn_fwd",
    )(seg, bias, q, k, v, tiles)


def attn_bwd_kernel(
    seg_ref, bias_ref, q_ref, k_ref, v_ref, o_ref, do_ref, lse_ref, tile_ref,
    dq_ref, dk_ref, dv_ref, near_ref, far_ref,
    s_ref, dp_ref, p_ref, ds_ref, dsum_ref, kt_ref, dqt_ref, dka_ref, dva_ref,
):
    length, width = q_ref.shape
    heads = width // 64
    lane = lax.broadcasted_iota(jnp.int32, (1, width), 1)
    one_example = seg_ref[0, length - 1] == seg_ref[0, 0]
    kt_ref[...] = jnp.transpose(k_ref[...])
    prod = o_ref[...].astype(F32) * do_ref[...].astype(F32)
    high = prod.astype(BF16)
    low = (prod - high.astype(F32)).astype(BF16)
    head_rows = (
        lax.broadcasted_iota(jnp.int32, (8 * heads, width), 1) // 64
        == lax.broadcasted_iota(jnp.int32, (8 * heads, width), 0) // 8
    ).astype(BF16)
    dsum_ref[...] = lax.dot_general(head_rows, high, NT, preferred_element_type=F32) + lax.dot_general(
        head_rows, low, NT, preferred_element_type=F32
    )
    NN = (((1,), (0,)), ((), ()))

    def blocks(h, mask, spans):
        below = bias_ref[15, h]
        above = bias_ref[31, h]
        near_sum = [None, None, None]
        far_sum = [jnp.zeros((8, TILE), F32)] * 2
        zero = jnp.zeros((), BF16)
        for d in range(3):
            near_ref[h, d] = jnp.zeros((TILE, TILE), F32)
        for lo, hi in spans:
            qh = jnp.where(mask, q_ref[lo:hi], zero)
            dh = jnp.where(mask, do_ref[lo:hi], zero)
            s_ref[lo:hi, lo:hi] = lax.dot_general(k_ref[lo:hi], qh, NT, preferred_element_type=F32)
            dp_ref[lo:hi, lo:hi] = lax.dot_general(v_ref[lo:hi], dh, NT, preferred_element_type=F32)
            for i in range(lo // TILE, hi // TILE):
                cols = slice(i * TILE, (i + 1) * TILE)
                lse = lse_ref[h, 0:1, cols]
                dsum = dsum_ref[pl.ds(pl.multiple_of(h * 8, 8), 1), cols]
                for j in range(lo // TILE, hi // TILE):
                    rows = slice(j * TILE, (j + 1) * TILE)
                    s = s_ref[rows, cols]
                    if abs(j - i) <= 1:
                        e = jnp.exp(s + tile_ref[h, j - i + 1] - lse)
                    else:
                        e = jnp.exp(s - (lse - (below if j < i else above)))
                    ds = e * (dp_ref[rows, cols] - dsum)
                    p_ref[rows, cols] = e.astype(BF16)
                    ds_ref[rows, cols] = ds.astype(BF16)
                    if abs(j - i) <= 1:
                        near_ref[h, j - i + 1] += ds
                    else:
                        side = int(j > i)
                        far_sum[side] = far_sum[side] + jnp.sum(ds.reshape(TILE // 8, 8, TILE), axis=0)
            dv = lax.dot_general(p_ref[lo:hi, lo:hi], dh, NN, preferred_element_type=F32)
            dk = lax.dot_general(ds_ref[lo:hi, lo:hi], qh, NN, preferred_element_type=F32)
            dva_ref[lo:hi] = jnp.where(mask, dv, dva_ref[lo:hi])
            dka_ref[lo:hi] = jnp.where(mask, dk, dka_ref[lo:hi])
            head = pl.ds(pl.multiple_of(h * 64, 64), 64)
            dqt_ref[head, lo:hi] = lax.dot_general(
                kt_ref[head, lo:hi], ds_ref[lo:hi, lo:hi], NN, preferred_element_type=F32
            )
        far_ref[h, 0] = far_sum[0]
        far_ref[h, 1] = far_sum[1]

    @pl.loop(0, heads)
    def _(h):
        mask = (lane // 64) == h

        @pl.when(one_example)
        def _():
            blocks(h, mask, ((0, length),))

        @pl.when(jnp.logical_not(one_example))
        def _():
            blocks(h, mask, tuple((lo, lo + SEG) for lo in range(0, length, SEG)))

    dk_ref[...] = dka_ref[...].astype(BF16)
    dv_ref[...] = dva_ref[...].astype(BF16)
    dq_ref[...] = jnp.transpose(dqt_ref[...]).astype(BF16)


def attn_bwd(seg, bias, q, k, v, o, do, lse, tiles):
    length, width = q.shape
    heads = width // 64
    vmem = pl.BlockSpec(memory_space=pltpu.VMEM)
    smem = pl.BlockSpec(memory_space=pltpu.SMEM)
    grad = jax.ShapeDtypeStruct((length, width), BF16)
    return pl.pallas_call(
        attn_bwd_kernel,
        out_shape=(
            grad, grad, grad,
            jax.ShapeDtypeStruct((heads, 3, TILE, TILE), F32),
            jax.ShapeDtypeStruct((heads, 2, 8, TILE), F32),
        ),
        in_specs=[smem, smem] + [vmem] * 7,
        out_specs=(vmem,) * 5,
        scratch_shapes=[
            pltpu.VMEM((length, length), F32),
            pltpu.VMEM((length, length), F32),
            pltpu.VMEM((length, length), BF16),
            pltpu.VMEM((length, length), BF16),
            pltpu.VMEM((8 * heads, length), F32),
            pltpu.VMEM((width, length), BF16),
            pltpu.VMEM((width, length), F32),
            pltpu.VMEM((length, width), F32),
            pltpu.VMEM((length, width), F32),
        ],
        compiler_params=pltpu.CompilerParams(vmem_limit_bytes=48 << 20),
        cost_estimate=pl.CostEstimate(flops=40_000_000_000, bytes_accessed=6_000_000, transcendentals=5_000_000),
        name="attn_bwd",
    )(seg, bias, q, k, v, o, do, lse, tiles)


def rms_norm(values, gain):
    return values * lax.rsqrt(jnp.mean(values * values, axis=-1, keepdims=True) + EPSILON) * gain


def norm_back(values, gain, grad):
    _, back_fn = jax.vjp(rms_norm, values, gain)
    return back_fn(grad)


def gelu_mix(gate_preactivation, upward_preactivation):
    return jax.nn.gelu(gate_preactivation, approximate=True) * upward_preactivation


def local(
    tokens,
    segment_ids,
    norm1_gain,
    w_query,
    w_key,
    w_value,
    w_out,
    rel_bias,
    norm2_gain,
    gate_weight_matrix,
    upward_weight,
    downward_weight,
    cotangent,
):
    shard_len, rows_here, model_width = tokens.shape
    length = segment_ids.shape[1]
    num_buckets, heads_here = rel_bias.shape
    head_dim = w_query.shape[1] // heads_here
    row_tiles, col_tiles = bias_tiles(rel_bias)
    x_in = tokens.astype(jnp.float32)
    norm_one = rms_norm(x_in, norm1_gain).astype(jnp.bfloat16)
    full_one = lax.all_gather(norm_one, "tensor", axis=0, tiled=True)

    def project(weight):
        return jnp.einsum(
            "trd,dc->rtc", full_one, weight, preferred_element_type=jnp.float32
        ).astype(jnp.bfloat16)

    q = project(w_query)
    k = project(w_key)
    v = project(w_value)
    mixed, lse = attn_fwd(segment_ids, rel_bias, q[0], k[0], v[0], row_tiles)
    mixed_flat = mixed[None]
    portion = lax.slice_in_dim(mixed_flat, 0, shard_len * lax.axis_size("tensor"), axis=1)
    attn_sum = lax.psum_scatter(
        jnp.einsum("rtc,cd->trd", portion, w_out, preferred_element_type=jnp.float32).astype(
            jnp.bfloat16
        ),
        "tensor",
        scatter_dimension=0,
        tiled=True,
    ).astype(jnp.float32)
    hidden_in = x_in + attn_sum
    norm_two = rms_norm(hidden_in, norm2_gain).astype(jnp.bfloat16)
    whole_second = lax.all_gather(norm_two, "tensor", axis=0, tiled=True)
    gate_preactivation = jnp.einsum(
        "hzo,on->hzn", whole_second, gate_weight_matrix, preferred_element_type=jnp.float32
    )
    upward_preactivation = jnp.einsum(
        "hzo,on->hzn", whole_second, upward_weight, preferred_element_type=jnp.float32
    )
    hidden_state = gelu_mix(gate_preactivation, upward_preactivation).astype(jnp.bfloat16)
    portion = lax.slice_in_dim(hidden_state, 0, lax.axis_size("tensor") * shard_len, axis=0)
    ffn_sum = lax.psum_scatter(
        jnp.einsum(
            "kwc,cn->kwn", portion, downward_weight, preferred_element_type=jnp.float32
        ).astype(jnp.bfloat16),
        "tensor",
        scatter_dimension=0,
        tiled=True,
    ).astype(jnp.float32)
    out_value = hidden_in + ffn_sum
    out_tokens = out_value.astype(jnp.bfloat16)
    stat_parts = jnp.stack(
        [jnp.sum(attn_sum * attn_sum), jnp.sum(ffn_sum * ffn_sum), jnp.sum(out_value * out_value)]
    )
    _, mix_back = jax.vjp(gelu_mix, gate_preactivation, upward_preactivation)
    cotangent_whole = lax.all_gather(cotangent, "tensor", axis=0, tiled=True)
    downward_weight_gradient = jnp.einsum(
        "kpo,kpb->ob", hidden_state, cotangent_whole, preferred_element_type=jnp.float32
    )
    hidden_gradient = jnp.einsum(
        "gqm,zm->gqz", cotangent_whole, downward_weight, preferred_element_type=jnp.float32
    )
    d_gate_f, d_up_f = mix_back(hidden_gradient)
    gate_gradient = d_gate_f.astype(jnp.bfloat16)
    upward_gradient = d_up_f.astype(jnp.bfloat16)
    gate_weight_gradient = jnp.einsum(
        "zyv,zya->va", whole_second, gate_gradient, preferred_element_type=jnp.float32
    )
    upward_weight_gradient = jnp.einsum(
        "zyv,zya->va", whole_second, upward_gradient, preferred_element_type=jnp.float32
    )
    row_count = lax.axis_size("tensor") * shard_len
    gate_portion = lax.slice_in_dim(gate_gradient, 0, row_count, axis=0)
    upward_portion = lax.slice_in_dim(upward_gradient, 0, row_count, axis=0)
    d_norm_two = lax.psum_scatter(
        (
            jnp.einsum(
                "xas,ks->xak", gate_portion, gate_weight_matrix, preferred_element_type=jnp.float32
            )
            + jnp.einsum(
                "xas,ks->xak", upward_portion, upward_weight, preferred_element_type=jnp.float32
            )
        ).astype(jnp.bfloat16),
        "tensor",
        scatter_dimension=0,
        tiled=True,
    ).astype(jnp.float32)
    d_from_two, grad_two_part = norm_back(hidden_in, norm2_gain, d_norm_two)
    d_hidden_in = cotangent.astype(jnp.float32) + d_from_two
    d_attn = d_hidden_in.astype(jnp.bfloat16)
    d_attn_full = lax.all_gather(d_attn, "tensor", axis=0, tiled=True)
    grad_out = jnp.einsum(
        "rtc,trd->cd", mixed_flat, d_attn_full, preferred_element_type=jnp.float32
    )
    d_mixed = jnp.einsum(
        "trd,cd->rtc", d_attn_full, w_out, preferred_element_type=jnp.float32
    ).astype(jnp.bfloat16)
    dq, dk, dv, near, far = attn_bwd(
        segment_ids, rel_bias, q[0], k[0], v[0], mixed, d_mixed[0], lse, col_tiles
    )
    grad_bias = bias_grad(near, far)[:, :heads_here]
    dq_flat, dk_flat, dv_flat = dq[None], dk[None], dv[None]
    grad_query = jnp.einsum("trd,rtc->dc", full_one, dq_flat, preferred_element_type=jnp.float32)
    grad_key = jnp.einsum("trd,rtc->dc", full_one, dk_flat, preferred_element_type=jnp.float32)
    grad_value = jnp.einsum("trd,rtc->dc", full_one, dv_flat, preferred_element_type=jnp.float32)
    row_count = lax.axis_size("tensor") * shard_len
    term_sum = jnp.einsum(
        "rtc,dc->trd",
        lax.slice_in_dim(dq_flat, 0, row_count, axis=1),
        w_query,
        preferred_element_type=jnp.float32,
    )
    term_sum = term_sum + jnp.einsum(
        "rtc,dc->trd",
        lax.slice_in_dim(dk_flat, 0, row_count, axis=1),
        w_key,
        preferred_element_type=jnp.float32,
    )
    d_norm_one = lax.psum_scatter(
        (
            term_sum
            + jnp.einsum(
                "rtc,dc->trd",
                lax.slice_in_dim(dv_flat, 0, row_count, axis=1),
                w_value,
                preferred_element_type=jnp.float32,
            )
        ).astype(jnp.bfloat16),
        "tensor",
        scatter_dimension=0,
        tiled=True,
    ).astype(jnp.float32)
    d_from_one, grad_one_part = norm_back(x_in, norm1_gain, d_norm_one)
    grad_tokens = (d_hidden_in + d_from_one).astype(jnp.bfloat16)
    big = (
        grad_query,
        grad_key,
        grad_value,
        grad_out,
        gate_weight_gradient,
        upward_weight_gradient,
        downward_weight_gradient,
    )
    big = lax.psum(tuple(g.astype(jnp.bfloat16) for g in big), "dp")
    (
        grad_query,
        grad_key,
        grad_value,
        grad_out,
        gate_weight_gradient,
        upward_weight_gradient,
        downward_weight_gradient,
    ) = (g.astype(jnp.float32) for g in big)
    grad_bias = lax.psum(grad_bias, "dp")
    grad_norm1, grad_norm2, stat_sums = lax.psum(
        (grad_one_part, grad_two_part, stat_parts), ("dp", "tensor")
    )
    element_count = (
        shard_len * rows_here * model_width * lax.axis_size("dp") * lax.axis_size("tensor")
    )
    rms_stats = jnp.sqrt(stat_sums / element_count)
    return (
        out_tokens,
        grad_tokens,
        grad_norm1,
        grad_query,
        grad_key,
        grad_value,
        grad_out,
        grad_bias,
        grad_norm2,
        gate_weight_gradient,
        upward_weight_gradient,
        downward_weight_gradient,
        rms_stats,
    )


def solution(mesh):
    in_specs = (
        P("tensor", "dp", None),
        P("dp", None),
        P(),
        P(None, "tensor"),
        P(None, "tensor"),
        P(None, "tensor"),
        P("tensor", None),
        P(None, "tensor"),
        P(),
        P(None, "tensor"),
        P(None, "tensor"),
        P("tensor", None),
        P("tensor", "dp", None),
    )
    out_specs = (
        P("tensor", "dp", None),
        P("tensor", "dp", None),
        P(),
        P(None, "tensor"),
        P(None, "tensor"),
        P(None, "tensor"),
        P("tensor", None),
        P(None, "tensor"),
        P(),
        P(None, "tensor"),
        P(None, "tensor"),
        P("tensor", None),
        P(),
    )
    return jax.shard_map(local, mesh=mesh, in_specs=in_specs, out_specs=out_specs, check_vma=False)
```

profile of v0, /device:TPU:0, one launch (start us, length us, event | category | flops | bytes accessed | tf_op | source)
XLA Modules:
  0.0 641.9 jit_solution(7237580738177401481)
XLA Ops:
  7.3 1.4 fusion.70
  8.7 2.1 fusion.61
  11.5 5.2 bias_tiles.1
  16.7 47.4 %all-gather.5.cloned.1.call-done = bf16[1152,1,1024]{2,0,1:T(8,128)(2,1)} async-done(((bf16[288,1,1024]{2,0,1:T(8,128)(2,1)}), bf16[1152,1,1024]{2,0,1:T(8,128)(2,1)}) %all-gather.5.cloned.1.call-update) | async-done | bytes 2359312 | tf_op jit(solution)/shard_map/all_gather | solution.py:316
  64.1 2.6 convolution_convert_fusion.4.k_ref
  69.2 7.7 %attn_fwd.1 = (bf16[1152,256]{1,0:T(8,128)(2,1)S(1)}, f32[4,8,1152]{2,1,0:T(8,128)S(1)}) custom-call(s32[1,1152]{1,0:T(1,128)S(1)} %copy-done.6, f32[32,4]{1,0:T(8,128)S(1)} %copy-done.3, bf16[1152,256]{1,0:T(8,128)(2,1)S(1)} %convolution_convert_fusion.5.q_ref, bf16[1152,256]{1,0:T(8,128)(2,1)S(1)} %convolution_convert_fusion.4.k_ref, ...), custom_call_target="tpu_custom_call" | custom-call | flops 20000000000 | bytes 4000000 | tf_op jit(solution)/shard_map/attn_fwd/pallas_call | solution.py:148
  76.9 2.2 fusion.2
  79.2 56.2 %reduce-scatter.5.cloned.1.call-done = bf16[288,1,1024]{2,0,1:T(8,128)(2,1)} async-done(((bf16[1152,1,1024]{2,0,1:T(8,128)(2,1)}), bf16[288,1,1024]{2,0,1:T(8,128)(2,1)}) %reduce-scatter.5.cloned.1.call-update) | async-done | bytes 589840 | tf_op jit(solution)/shard_map/reduce_scatter | solution.py:329
  135.4 1.3 multiply_reduce_fusion.1
  136.7 2.1 multiply_convert_fusion.2
  139.8 49.3 %all-gather.7.cloned.1.call-done = bf16[1152,1,1024]{2,0,1:T(8,128)(2,1)} async-done(((bf16[288,1,1024]{2,0,1:T(8,128)(2,1)}), bf16[1152,1,1024]{2,0,1:T(8,128)(2,1)}) %all-gather.7.cloned.1.call-update) | async-done | bytes 2359312 | tf_op jit(solution)/shard_map/all_gather | solution.py:339
  189.0 6.0 fusion.23
  195.0 3.7 fusion.25
  198.8 41.0 %all-gather.9.cloned.1.call-done = bf16[1152,1,1024]{2,0,1:T(8,128)(2,1)} async-done(((bf16[288,1,1024]{2,0,1:T(8,128)(2,1)}), bf16[1152,1,1024]{2,0,1:T(8,128)(2,1)}) %all-gather.9.cloned.1.call-update) | async-done | bytes 2359312 | tf_op jit(solution)/shard_map/all_gather | solution.py:362
  239.8 8.2 %multiply_convert_fusion = (bf16[1152,704]{0,1:T(8,128)(2,1)}, bf16[1152,704]{0,1:T(8,128)(2,1)}, bf16[1152,704]{0,1:T(8,128)(2,1)S(1)}) fusion(f32[1152,704]{0,1:T(8,128)} %fusion.25, f32[1152,704]{0,1:T(8,128)} %fusion.23, bf16[704,1024]{1,0:T(8,128)(2,1)S(1)} %copy-done, bf16[1152,1,1024]{2,0,1:T(8,128)(2,1)} %all-gather.9.cloned.1.call-done), kind=kOutput, calls=%fused_computation.19 | convolution fusion | flops 1682030592 | bytes 15155200 | tf_op jit(solution)/shard_map/gqm,zm->gqz/dot_general | solution.py:366
  248.0 1.2 copy-done.46
  249.1 3.5 fusion.1
  252.7 1.3 copy-done.41
  253.9 3.6 fusion.76
  257.6 3.6 fusion.4
  261.3 38.3 %reduce-scatter.7.cloned.1.call-done = bf16[288,1,1024]{2,0,1:T(8,128)(2,1)} async-done(((bf16[1152,1,1024]{2,0,1:T(8,128)(2,1)}), bf16[288,1,1024]{2,0,1:T(8,128)(2,1)}) %reduce-scatter.7.cloned.1.call-update) | async-done | bytes 589840 | tf_op jit(solution)/shard_map/reduce_scatter | solution.py:348
  299.6 50.3 %reduce-scatter.9.cloned.1.call-done = bf16[288,1,1024]{2,0,1:T(8,128)(2,1)} async-done(((bf16[1152,1,1024]{2,0,1:T(8,128)(2,1)}), bf16[288,1,1024]{2,0,1:T(8,128)(2,1)}) %reduce-scatter.9.cloned.1.call-update) | async-done | bytes 589840 | tf_op jit(solution)/shard_map/reduce_scatter | solution.py:381
  349.9 3.5 fusion.65
  353.4 1.3 fusion.75
  354.8 9.8 %all-reduce.4.cloned.1.call-start = ((), (), s32[]{:S(2)}) async-start(), calls=%async_computation.12 | async-start | bytes 12845056 | tf_op jit(solution)/shard_map/psum | solution.py:450
  364.6 5.5 fusion.42
  370.1 3.1 fusion.36
  373.2 3.1 fusion.39
  376.3 28.6 %all-gather.11.cloned.1.call-done = bf16[1152,1,1024]{2,0,1:T(8,128)(2,1)} async-done(((bf16[288,1,1024]{2,0,1:T(8,128)(2,1)}), bf16[1152,1,1024]{2,0,1:T(8,128)(2,1)}) %all-gather.11.cloned.1.call-update) | async-done | bytes 2359312 | tf_op jit(solution)/shard_map/all_gather | solution.py:397
  404.9 2.6 convolution_convert_fusion.2.do_ref
  407.5 8.7 %attn_bwd.1 = (bf16[1152,256]{1,0:T(8,128)(2,1)S(1)}, bf16[1152,256]{1,0:T(8,128)(2,1)S(1)}, bf16[1152,256]{1,0:T(8,128)(2,1)S(1)}, f32[4,3,128,128]{3,2,1,0:T(8,128)S(1)}, f32[4,2,8,128]{3,2,1,0:T(8,128)S(1)}) custom-call(s32[1,1152]{1,0:T(1,128)S(1)} %copy-done.6, f32[32,4]{1,0:T(8,128)S(1)} %copy-done.3, bf16[1152,256]{1,0:T(8,128)(2,1)S(1)} %copy-done.10, ...), custom_call_target="tpu_custom_call" | custom-call | flops 40000000000 | bytes 6000000 | tf_op jit(solution)/shard_map/attn_bwd/pallas_call | solution.py:255
  416.3 1.7 fusion.58
  418.4 1.7 fusion.49
  420.1 1.7 fusion.52
  421.8 1.7 fusion.55
  426.4 2.3 fusion.3
  428.8 2.0 pad_maximum_fusion
  430.8 3.6 bias_grad.1
  434.4 34.0 %psum.82 = f32[32,4]{1,0:T(8,128)S(1)} all-reduce(f32[32,4]{1,0:T(8,128)} %bitcast.96), channel_id=1, replica_groups=mesh['dp'=8,'tensor'=4] {'dp'}, use_global_device_ids=true, to_apply=%region_14.0 | all-reduce | flops 128 | bytes 1024 | tf_op jit(solution)/shard_map/psum | solution.py:460
  469.0 70.7 %all-reduce.4.cloned.1.call-done = (bf16[1024,256]{1,0:T(8,128)(2,1)}, bf16[1024,256]{1,0:T(8,128)(2,1)}, bf16[1024,256]{1,0:T(8,128)(2,1)}, bf16[256,1024]{1,0:...) async-done(((bf16[1024,256]{1,0:T(8,128)(2,1)}, bf16[1024,256]{1,0:T(8,128)(2,1)}, bf16[1024,256]{1,0:T(8,128)(2,1)}, ...) | async-done | bytes 6422544 | tf_op jit(solution)/shard_map/psum | solution.py:450
  539.7 2.2 convert_element_type.171
  545.1 1.9 convert_element_type.179
  547.0 1.9 convert_element_type.181
  549.0 1.9 convert_element_type.183
  550.9 39.3 %reduce-scatter.11.cloned.1.call-done = bf16[288,1,1024]{2,0,1:T(8,128)(2,1)} async-done(((bf16[1152,1,1024]{2,0,1:T(8,128)(2,1)}), bf16[288,1,1024]{2,0,1:T(8,128)(2,1)}) %reduce-scatter.11.cloned.1.call-update) | async-done | bytes 589840 | tf_op jit(solution)/shard_map/reduce_scatter | solution.py:425
  590.2 1.6 fusion.66
  591.8 39.9 %all-reduce = (f32[1024]{0:T(1024)}, f32[1024]{0:T(1024)}, f32[3]{0:T(128)S(1)}) all-reduce(f32[1024]{0:T(1024)S(1)} %get-tuple-element.47, f32[1024]{0:T(1024)S(1)} %get-tuple-element.44, f32[3]{0:T(128)S(1)} %pad_maximum_fusion), channel_id=1, replica_groups=mesh['dp'=8,'tensor'=4] {'dp','tensor'}, use_global_device_ids=true, to_apply=%region_9.0 | all-reduce | flops 2051 | bytes 16408 | tf_op jit(solution)/shard_map/psum | solution.py:461
  632.3 2.8 fusion.69
  (123 shorter events, 12.1 us)
Async XLA Ops:
  7.2 232.6 %copy-start = (bf16[704,1024]{1,0:T(8,128)(2,1)S(1)}, bf16[704,1024]{1,0:T(8,128)(2,1)}, u32[]{:S(2)}) copy-start(bf16[704,1024]{1,0:T(8,128)(2,1)} %param.24) | copy-start | bytes 4325380
  7.2 3.6 copy-start.35
  7.2 56.9 %copy-start.24 = (bf16[1024,256]{1,0:T(8,128)(2,1)S(1)}, bf16[1024,256]{1,0:T(8,128)(2,1)}, u32[]{:S(2)}) copy-start(bf16[1024,256]{1,0:T(8,128)(2,1)} %param.17) | copy-start | bytes 1572868
  7.2 56.9 %all-gather.5.cloned.1.call-start = ((), (), s32[]{:S(2)}) async-start(), calls=%async_computation.4 | async-start | bytes 2949120 | tf_op jit(solution)/shard_map/all_gather | solution.py:316
  10.8 124.6 %reduce-scatter.5.cloned.1.call-start = ((), (), s32[]{:S(2)}) async-start(), calls=%async_computation.5 | async-start | bytes 2949120 | tf_op jit(solution)/shard_map/reduce_scatter | solution.py:329
  16.7 50.0 %copy-start.26 = (bf16[1024,256]{1,0:T(8,128)(2,1)S(1)}, bf16[1024,256]{1,0:T(8,128)(2,1)}, u32[]{:S(2)}) copy-start(bf16[1024,256]{1,0:T(8,128)(2,1)} %param.18) | copy-start | bytes 1572868
  64.1 2.6 copy-start.36
  68.6 8.3 %copy-start.9 = (bf16[1152,256]{1,0:T(8,128)(2,1)}, bf16[1152,256]{1,0:T(8,128)(2,1)S(1)}, u32[]{:S(2)}) copy-start(bf16[1152,256]{1,0:T(8,128)(2,1)S(1)} %convolution_convert_fusion.5.q_ref) | copy-start | bytes 1769476
  69.2 7.7 %copy-start.31 = (bf16[256,1024]{1,0:T(8,128)(2,1)S(1)}, bf16[256,1024]{1,0:T(8,128)(2,1)}, u32[]{:S(2)}) copy-start(bf16[256,1024]{1,0:T(8,128)(2,1)} %param.19) | copy-start | bytes 1572868
  79.1 56.3 %copy-start.11 = (bf16[288,1,1024]{2,0,1:T(8,128)(2,1)S(1)}, bf16[288,1,1024]{2,0,1:T(8,128)(2,1)}, u32[]{:S(2)}) copy-start(bf16[288,1,1024]{2,0,1:T(8,128)(2,1)} %param.13) | copy-start | bytes 1769476
  79.1 57.6 %copy-start.33 = (f32[1024]{0:T(1024)S(1)}, f32[1024]{0:T(1024)}, u32[]{:S(2)}) copy-start(f32[1024]{0:T(1024)} %param.21) | copy-start | bytes 12292
  79.1 109.9 %all-gather.7.cloned.1.call-start = ((), (), s32[]{:S(2)}) async-start(), calls=%async_computation.6 | async-start | bytes 2949120 | tf_op jit(solution)/shard_map/all_gather | solution.py:339
  138.9 100.9 %all-gather.9.cloned.1.call-start = ((), (), s32[]{:S(2)}) async-start(), calls=%async_computation.8 | async-start | bytes 2949120 | tf_op jit(solution)/shard_map/all_gather | solution.py:362
  139.5 160.2 %reduce-scatter.7.cloned.1.call-start = ((), (), s32[]{:S(2)}) async-start(), calls=%async_computation.7 | async-start | bytes 2949120 | tf_op jit(solution)/shard_map/reduce_scatter | solution.py:348
  189.0 6.0 copy-start.38
  189.0 6.0 copy-start.40
  252.6 1.4 copy-start.41
  252.6 97.3 %reduce-scatter.9.cloned.1.call-start = ((), (), s32[]{:S(2)}) async-start(), calls=%async_computation.9 | async-start | bytes 2949120 | tf_op jit(solution)/shard_map/reduce_scatter | solution.py:381
  253.9 3.6 copy-start.42
  253.9 3.6 copy-start.44
  261.2 88.7 %copy-start.13 = (bf16[288,1,1024]{2,0,1:T(8,128)(2,1)S(1)}, bf16[288,1,1024]{2,0,1:T(8,128)(2,1)}, u32[]{:S(2)}) copy-start(bf16[288,1,1024]{2,0,1:T(8,128)(2,1)} %reduce-scatter.5.cloned.1.call-done) | copy-start | bytes 1769476
  261.2 92.2 %copy-start.15 = (bf16[288,1,1024]{2,0,1:T(8,128)(2,1)S(1)}, bf16[288,1,1024]{2,0,1:T(8,128)(2,1)}, u32[]{:S(2)}) copy-start(bf16[288,1,1024]{2,0,1:T(8,128)(2,1)} %param.25) | copy-start | bytes 1769476
  261.3 143.6 %all-gather.11.cloned.1.call-start = ((), (), s32[]{:S(2)}) async-start(), calls=%async_computation.10 | async-start | bytes 2949120 | tf_op jit(solution)/shard_map/all_gather | solution.py:397
  349.9 3.5 copy-start.17
  354.8 185.0 %all-reduce.4.cloned.1.call-start = ((), (), s32[]{:S(2)}) async-start(), calls=%async_computation.12 | async-start | bytes 12845056 | tf_op jit(solution)/shard_map/psum | solution.py:450
  364.5 5.5 copy-start.39
  364.5 5.5 copy-start.45
  370.1 3.1 copy-start.43
  373.2 31.7 %copy-start.32 = (bf16[256,1024]{1,0:T(8,128)(2,1)S(1)}, bf16[256,1024]{1,0:T(8,128)(2,1)}, u32[]{:S(2)}) copy-start(bf16[256,1024]{1,0:T(8,128)(2,1)} %param.19) | copy-start | bytes 1572868
  404.9 2.6 copy-start.8
  404.9 2.6 copy-start.10
  407.5 8.7 %copy-start.18 = (bf16[1152,1,1024]{2,0,1:T(8,128)(2,1)S(1)}, bf16[1152,1,1024]{2,0,1:T(8,128)(2,1)}, u32[]{:S(2)}) copy-start(bf16[1152,1,1024]{2,0,1:T(8,128)(2,1)} %all-gather.11.cloned.1.call-done) | copy-start | bytes 7077892
  416.3 1.7 copy-start.2
  416.3 1.7 copy-start.4
  416.3 2.1 copy-start.37
  423.6 1.8 copy-start.25
  423.6 166.7 %reduce-scatter.11.cloned.1.call-start = ((), (), s32[]{:S(2)}) async-start(), calls=%async_computation.11 | async-start | bytes 2949120 | tf_op jit(solution)/shard_map/reduce_scatter | solution.py:425
  539.7 2.2 copy-start.30
  539.7 3.2 copy-start.29
  541.9 2.1 copy-start.28
  542.9 2.1 copy-start.21
  545.1 1.9 copy-start.20
  547.0 1.9 copy-start.19
  549.0 41.3 %copy-start.12 = (bf16[288,1,1024]{2,0,1:T(8,128)(2,1)S(1)}, bf16[288,1,1024]{2,0,1:T(8,128)(2,1)}, u32[]{:S(2)}) copy-start(bf16[288,1,1024]{2,0,1:T(8,128)(2,1)} %param.13) | copy-start | bytes 1769476
  549.0 41.3 %copy-start.34 = (f32[1024]{0:T(1024)S(1)}, f32[1024]{0:T(1024)}, u32[]{:S(2)}) copy-start(f32[1024]{0:T(1024)} %param.15) | copy-start | bytes 12292
  549.0 83.3 %copy-start.14 = (bf16[288,1,1024]{2,0,1:T(8,128)(2,1)S(1)}, bf16[288,1,1024]{2,0,1:T(8,128)(2,1)}, u32[]{:S(2)}) copy-start(bf16[288,1,1024]{2,0,1:T(8,128)(2,1)} %reduce-scatter.5.cloned.1.call-done) | copy-start | bytes 1769476
  549.0 83.3 %copy-start.16 = (bf16[288,1,1024]{2,0,1:T(8,128)(2,1)S(1)}, bf16[288,1,1024]{2,0,1:T(8,128)(2,1)}, u32[]{:S(2)}) copy-start(bf16[288,1,1024]{2,0,1:T(8,128)(2,1)} %param.25) | copy-start | bytes 1769476
  631.7 3.4 copy-start.1
  (8 other events, 8.6 us)
Sparse Core Ops, SparseCore 0:
  10.9 53.1 all-gather.4
  79.2 56.0 reduce-scatter.4
  139.0 49.9 all-gather.6
  190.4 49.2 all-gather.8
  252.7 46.8 reduce-scatter.6
  302.3 47.4 reduce-scatter.8
  354.9 49.9 all-gather.10
  423.7 115.9 all-reduce.3
  542.0 48.1 reduce-scatter.10
where the time goes:
time: 651 us; the launch traced here: 642 us
  waiting for transfers between devices  422 us (65%)
  blocking collectives  73.9 us (11%)
  matrix products  60.1 us (9%)
  other arithmetic  29.9 us (5%)
  Pallas kernels  25.2 us (4%)
  between operations  14.4 us (2%)
  starting transfers between devices  10.6 us (2%)
    psum x1, waiting for transfers between devices, local(): big = lax.psum(tuple((g.astype(jnp.bfloat16) for g in big)), 'dp')  70.7 us
    reduce_scatter x1, waiting for transfers between devices, local(): lax.psum_scatter(jnp.einsum('rtc,cd->trd', portion, w_out, preferred_elem...  56.2 us
    reduce_scatter x1, waiting for transfers between devices, local(): lax.psum_scatter((jnp.einsum('xas,ks->xak', gate_portion, gate_weight_mat...  50.3 us
    all_gather x1, waiting for transfers between devices, local(): whole_second = lax.all_gather(norm_two, 'tensor', axis=0, tiled=True)  49.3 us
    all_gather x1, waiting for transfers between devices, local(): full_one = lax.all_gather(norm_one, 'tensor', axis=0, tiled=True)  47.4 us
    all_gather x1, waiting for transfers between devices, local(): cotangent_whole = lax.all_gather(cotangent, 'tensor', axis=0, tiled=True)  41 us
    psum x1, blocking collectives, local(): lax.psum((grad_one_part, grad_two_part, stat_parts), ('dp', 'tensor'))  39.9 us
    reduce_scatter x1, waiting for transfers between devices, local(): lax.psum_scatter((term_sum + jnp.einsum('rtc,dc->trd', lax.slice_in_dim(d...  39.3 us
  transfers between devices with their start and end apart: 9, of which 9 were waited for; matrix products, arithmetic and copies ran while one was open for 7% of the time, Pallas kernels for 1%

commit v1 on v0

--- a/solution.py
+++ b/solution.py
@@ -1,16 +1,17 @@
 import functools
-from jax.sharding import PartitionSpec as P
 import jax
 import jax.numpy as jnp
 from jax import lax
 from jax.experimental import pallas as pl
 from jax.experimental.pallas import tpu as pltpu
+from jax.sharding import PartitionSpec as P
 
 EPSILON = 1e-06
 THRESHOLDS = (12, 16, 23, 32, 46, 64, 91)
 TILE = 128
 SEG = 384
 NT = (((1,), (1,)), ((), ()))
+NN = (((1,), (0,)), ((), ()))
 TN = (((0,), (0,)), ((), ()))
 F32 = jnp.float32
 BF16 = jnp.bfloat16
@@ -82,8 +83,9 @@
     )(near, far)
 
 
-def attn_fwd_kernel(seg_ref, bias_ref, q_ref, k_ref, v_ref, tile_ref, o_ref, lse_ref, s_ref, p_ref, l_ref):
-    length, width = q_ref.shape
+def attn_fwd_kernel(seg_ref, bias_ref, qkv_ref, tile_ref, o_ref, lse_ref, s_ref, p_ref, l_ref):
+    length, width = o_ref.shape
+    q_ref, k_ref, v_ref = (qkv_ref.at[:, n * width : (n + 1) * width] for n in range(3))
     heads = width // 64
     n_tiles = length // TILE
     lane = lax.broadcasted_iota(jnp.int32, (1, width), 1)
@@ -140,8 +142,8 @@
             blocks(h, mask, tuple((lo, lo + SEG) for lo in range(0, length, SEG)))
 
 
-def attn_fwd(seg, bias, q, k, v, tiles):
-    length, width = q.shape
+def attn_fwd(seg, bias, qkv, tiles):
+    length, width = qkv.shape[0], qkv.shape[1] // 3
     heads = width // 64
     vmem = pl.BlockSpec(memory_space=pltpu.VMEM)
     smem = pl.BlockSpec(memory_space=pltpu.SMEM)
@@ -151,7 +153,7 @@
             jax.ShapeDtypeStruct((length, width), BF16),
             jax.ShapeDtypeStruct((heads, 8, length), F32),
         ),
-        in_specs=[smem, smem, vmem, vmem, vmem, vmem],
+        in_specs=[smem, smem, vmem, vmem],
         out_specs=(vmem, vmem),
         scratch_shapes=[
             pltpu.VMEM((length, length), F32),
@@ -161,15 +163,16 @@
         compiler_params=pltpu.CompilerParams(vmem_limit_bytes=40 << 20),
         cost_estimate=pl.CostEstimate(flops=20_000_000_000, bytes_accessed=4_000_000, transcendentals=5_000_000),
         name="attn_fwd",
-    )(seg, bias, q, k, v, tiles)
+    )(seg, bias, qkv, tiles)
 
 
 def attn_bwd_kernel(
-    seg_ref, bias_ref, q_ref, k_ref, v_ref, o_ref, do_ref, lse_ref, tile_ref,
-    dq_ref, dk_ref, dv_ref, near_ref, far_ref,
+    seg_ref, bias_ref, qkv_ref, o_ref, do_ref, lse_ref, tile_ref,
+    dqkv_ref, near_ref, far_ref,
     s_ref, dp_ref, p_ref, ds_ref, dsum_ref, kt_ref, dqt_ref, dka_ref, dva_ref,
 ):
-    length, width = q_ref.shape
+    length, width = o_ref.shape
+    q_ref, k_ref, v_ref = (qkv_ref.at[:, n * width : (n + 1) * width] for n in range(3))
     heads = width // 64
     lane = lax.broadcasted_iota(jnp.int32, (1, width), 1)
     one_example = seg_ref[0, length - 1] == seg_ref[0, 0]
@@ -184,8 +187,6 @@
     dsum_ref[...] = lax.dot_general(head_rows, high, NT, preferred_element_type=F32) + lax.dot_general(
         head_rows, low, NT, preferred_element_type=F32
     )
-    NN = (((1,), (0,)), ((), ()))
-
     def blocks(h, mask, spans):
         below = bias_ref[15, h]
         above = bias_ref[31, h]
@@ -241,26 +242,25 @@
         def _():
             blocks(h, mask, tuple((lo, lo + SEG) for lo in range(0, length, SEG)))
 
-    dk_ref[...] = dka_ref[...].astype(BF16)
-    dv_ref[...] = dva_ref[...].astype(BF16)
-    dq_ref[...] = jnp.transpose(dqt_ref[...]).astype(BF16)
-
-
-def attn_bwd(seg, bias, q, k, v, o, do, lse, tiles):
-    length, width = q.shape
+    dqkv_ref[:, :width] = jnp.transpose(dqt_ref[...]).astype(BF16)
+    dqkv_ref[:, width : 2 * width] = dka_ref[...].astype(BF16)
+    dqkv_ref[:, 2 * width :] = dva_ref[...].astype(BF16)
+
+
+def attn_bwd(seg, bias, qkv, o, do, lse, tiles):
+    length, width = o.shape
     heads = width // 64
     vmem = pl.BlockSpec(memory_space=pltpu.VMEM)
     smem = pl.BlockSpec(memory_space=pltpu.SMEM)
-    grad = jax.ShapeDtypeStruct((length, width), BF16)
     return pl.pallas_call(
         attn_bwd_kernel,
         out_shape=(
-            grad, grad, grad,
+            jax.ShapeDtypeStruct((length, 3 * width), BF16),
             jax.ShapeDtypeStruct((heads, 3, TILE, TILE), F32),
             jax.ShapeDtypeStruct((heads, 2, 8, TILE), F32),
         ),
-        in_specs=[smem, smem] + [vmem] * 7,
-        out_specs=(vmem,) * 5,
+        in_specs=[smem, smem] + [vmem] * 5,
+        out_specs=(vmem,) * 3,
         scratch_shapes=[
             pltpu.VMEM((length, length), F32),
             pltpu.VMEM((length, length), F32),
@@ -275,20 +275,247 @@
         compiler_params=pltpu.CompilerParams(vmem_limit_bytes=48 << 20),
         cost_estimate=pl.CostEstimate(flops=40_000_000_000, bytes_accessed=6_000_000, transcendentals=5_000_000),
         name="attn_bwd",
-    )(seg, bias, q, k, v, o, do, lse, tiles)
-
-
-def rms_norm(values, gain):
-    return values * lax.rsqrt(jnp.mean(values * values, axis=-1, keepdims=True) + EPSILON) * gain
-
-
-def norm_back(values, gain, grad):
-    _, back_fn = jax.vjp(rms_norm, values, gain)
-    return back_fn(grad)
-
-
-def gelu_mix(gate_preactivation, upward_preactivation):
-    return jax.nn.gelu(gate_preactivation, approximate=True) * upward_preactivation
+    )(seg, bias, qkv, o, do, lse, tiles)
+
+
+def tanh_gelu(u):
+    scale = 0.7978845608028654
+    t = jnp.tanh(scale * (u + 0.044715 * (u * u * u)))
+    half = 0.5 * (1.0 + t)
+    slope = half + (0.5 * u) * (1.0 - t * t) * (scale * (1.0 + 0.134145 * (u * u)))
+    return u * half, slope
+
+
+def ffn_kernel(
+    where_ref, x_ref, c_ref, mine_ref, other_ref,
+    dtwo_ref, ffo_ref, hidden_ref, dgate_ref, dup_ref,
+    gate_w, up_w, down_w, sems,
+):
+    core = where_ref[0]
+    ring, rows, half = mine_ref.shape
+    units = rows // 3
+    scratches = (gate_w, up_w, down_w)
+    copies = [[], [], []]
+    for m in range(3):
+        for q in range(ring):
+            for n, ref in enumerate((mine_ref, other_ref)):
+                start = pl.multiple_of((core ^ n) * half, 128)
+                copies[m].append(
+                    pltpu.make_async_copy(
+                        ref.at[q, m * units : (m + 1) * units],
+                        scratches[m].at[q * units : (q + 1) * units, pl.ds(start, half)],
+                        sems.at[m, 2 * q + n],
+                    )
+                )
+    for group in copies:
+        for copy in group:
+            copy.start()
+    for copy in copies[0]:
+        copy.wait()
+    gate = lax.dot_general(x_ref[...], gate_w[...], NT, preferred_element_type=F32)
+    for copy in copies[1]:
+        copy.wait()
+    up = lax.dot_general(x_ref[...], up_w[...], NT, preferred_element_type=F32)
+    for copy in copies[2]:
+        copy.wait()
+    d_hidden = lax.dot_general(c_ref[...], down_w[...], NT, preferred_element_type=F32)
+    value, slope = tanh_gelu(gate)
+    hidden = (value * up).astype(BF16)
+    d_gate = (d_hidden * up * slope).astype(BF16)
+    d_up = (d_hidden * value).astype(BF16)
+    hidden_ref[...] = hidden
+    dgate_ref[...] = d_gate
+    dup_ref[...] = d_up
+    dtwo_ref[...] = (
+        lax.dot_general(d_gate, gate_w[...], NN, preferred_element_type=F32)
+        + lax.dot_general(d_up, up_w[...], NN, preferred_element_type=F32)
+    ).astype(dtwo_ref.dtype)
+    ffo_ref[...] = lax.dot_general(hidden, down_w[...], NN, preferred_element_type=F32).astype(ffo_ref.dtype)
+
+
+def ffn(where, x, c, mine, other):
+    tokens, width = x.shape
+    ring, rows, half = mine.shape
+    units = ring * rows // 3
+    vmem = pl.BlockSpec(memory_space=pltpu.VMEM)
+    anywhere = pl.BlockSpec(memory_space=pl.ANY)
+    wide = jax.ShapeDtypeStruct((tokens, width), BF16)
+    inner = jax.ShapeDtypeStruct((tokens, units), BF16)
+    return pl.pallas_call(
+        ffn_kernel,
+        out_shape=(wide, wide, inner, inner, inner),
+        in_specs=[pl.BlockSpec(memory_space=pltpu.SMEM), vmem, vmem, anywhere, anywhere],
+        out_specs=(vmem,) * 5,
+        scratch_shapes=[pltpu.VMEM((units, width), BF16)] * 3 + [pltpu.SemaphoreType.DMA((3, 2 * ring))],
+        compiler_params=pltpu.CompilerParams(vmem_limit_bytes=40 << 20),
+        cost_estimate=pl.CostEstimate(
+            flops=16 * tokens * width * units, bytes_accessed=6 * units * width + 10 * tokens * width, transcendentals=tokens * units
+        ),
+        name="ffn",
+    )(where, x, c, mine, other)
+
+
+def ffn_grads_kernel(n, where_ref, *refs):
+    sources = [refs[i * n : (i + 1) * n] for i in range(5)]
+    keep_ref, give_ref = refs[5 * n : 5 * n + 2]
+    held = refs[5 * n + 2 : 5 * n + 7]
+    sems = refs[5 * n + 7]
+    core = where_ref[0]
+    ring, _, units, half = keep_ref.shape
+    rows = sources[0][0].shape[0]
+    copies = [
+        [
+            pltpu.make_async_copy(ref, target.at[j * rows : (j + 1) * rows], sems.at[i, j])
+            for j, ref in enumerate(group)
+        ]
+        for i, (group, target) in enumerate(zip(sources, held))
+    ]
+    for group in copies:
+        for copy in group:
+            copy.start()
+    waited = set()
+    for m, (lhs, rhs) in ((2, (0, 1)), (0, (2, 3)), (1, (4, 3))):
+        for i in (lhs, rhs):
+            if i not in waited:
+                waited.add(i)
+                for copy in copies[i]:
+                    copy.wait()
+        for n_half, out_ref in enumerate((give_ref, keep_ref)):
+            start = pl.multiple_of((core ^ (1 - n_half)) * half, 128)
+            grad = lax.dot_general(
+                held[lhs][...], held[rhs][:, pl.ds(start, half)], TN, preferred_element_type=F32
+            ).astype(BF16)
+            for q in range(ring):
+                out_ref[q, m] = grad[q * units : (q + 1) * units]
+
+
+def ffn_grads(where, hs, cs, gs, xs, us, ring):
+    rows, width = xs[0].shape
+    units = hs[0].shape[1]
+    n = len(xs)
+    vmem = pl.BlockSpec(memory_space=pltpu.VMEM)
+    anywhere = pl.BlockSpec(memory_space=pl.ANY)
+    shape = jax.ShapeDtypeStruct((ring, 3, units // ring, width // 2), BF16)
+    wide, inner = pltpu.VMEM((n * rows, width), BF16), pltpu.VMEM((n * rows, units), BF16)
+    return pl.pallas_call(
+        functools.partial(ffn_grads_kernel, n),
+        out_shape=(shape, shape),
+        in_specs=[pl.BlockSpec(memory_space=pltpu.SMEM)] + [anywhere] * (5 * n),
+        out_specs=(vmem, vmem),
+        scratch_shapes=[inner, wide, inner, wide, inner, pltpu.SemaphoreType.DMA((5, n))],
+        compiler_params=pltpu.CompilerParams(vmem_limit_bytes=48 << 20),
+        cost_estimate=pl.CostEstimate(
+            flops=6 * n * rows * width * units, bytes_accessed=4 * n * rows * width + 6 * n * rows * units, transcendentals=0
+        ),
+        name="ffn_grads",
+    )(where, *hs, *cs, *gs, *xs, *us)
+
+
+def place_kernel(masks, where_ref, own_ref, other_ref, gate_ref, up_ref, down_ref):
+    core, chip = where_ref[0], where_ref[1]
+    _, _, units, half = own_ref.shape
+    for m, out_ref in enumerate((gate_ref, up_ref, down_ref)):
+        for r, mask in enumerate(masks):
+            rows = pl.ds(pl.multiple_of((chip ^ mask) * units, 8), units)
+            for n, ref in enumerate((own_ref, other_ref)):
+                columns = pl.ds(pl.multiple_of((core ^ n) * half, 128), half)
+                out_ref[rows, columns] = ref[r, m].astype(F32)
+
+
+def place(where, own, other, masks):
+    _, _, units, half = own.shape
+    vmem = pl.BlockSpec(memory_space=pltpu.VMEM)
+    shape = jax.ShapeDtypeStruct((4 * units, 2 * half), F32)
+    return pl.pallas_call(
+        functools.partial(place_kernel, masks),
+        out_shape=(shape,) * 3,
+        in_specs=[pl.BlockSpec(memory_space=pltpu.SMEM), vmem, vmem],
+        out_specs=(vmem,) * 3,
+        compiler_params=pltpu.CompilerParams(vmem_limit_bytes=40 << 20),
+        cost_estimate=pl.CostEstimate(flops=0, bytes_accessed=12 * own.size * 2, transcendentals=0),
+        name="place",
+    )(where, own, other)
+
+
+def place_rows_kernel(masks, where_ref, pieces_ref, *out_refs):
+    _, rows, width = pieces_ref.shape
+    part = width // len(out_refs)
+    for r, mask in enumerate(masks):
+        target = pl.ds(pl.multiple_of((where_ref[2] ^ mask) * rows, 8), rows)
+        value = pieces_ref[r].astype(F32)
+        for i, out_ref in enumerate(out_refs):
+            out_ref[target] = value[:, i * part : (i + 1) * part]
+
+
+def place_rows(where, pieces, masks, n_out):
+    count, rows, width = pieces.shape
+    vmem = pl.BlockSpec(memory_space=pltpu.VMEM)
+    return pl.pallas_call(
+        functools.partial(place_rows_kernel, masks),
+        out_shape=(jax.ShapeDtypeStruct((count * rows, width // n_out), F32),) * n_out,
+        in_specs=[pl.BlockSpec(memory_space=pltpu.SMEM), vmem],
+        out_specs=(vmem,) * n_out,
+        cost_estimate=pl.CostEstimate(flops=0, bytes_accessed=6 * pieces.size, transcendentals=0),
+        name="place_rows",
+    )(where, pieces)
+
+
+def swap(value, mask):
+    size = lax.axis_size("dp")
+    return lax.ppermute(value, "dp", [(i, i ^ mask) for i in range(size)])
+
+
+def shift(value, step):
+    size = lax.axis_size("tensor")
+    return lax.ppermute(value, "tensor", [(i, (i + step) % size) for i in range(size)])
+
+
+def add(left, right):
+    return (left.astype(F32) + right.astype(F32)).astype(BF16)
+
+
+def after(value, *others):
+    return lax.optimization_barrier((value, *others))[0]
+
+
+def bits_from(first):
+    bit = first
+    while bit < lax.axis_size("dp"):
+        yield bit
+        bit *= 2
+
+
+def gather_all(piece):
+    pieces, masks = piece[None], [0]
+    for bit in (*bits_from(2), 1):
+        pieces = jnp.concatenate([pieces, swap(pieces, bit)], axis=0)
+        masks = masks + [mask | bit for mask in masks]
+    return pieces, tuple(masks)
+
+
+def sum_rows(value):
+    for bit in bits_from(1):
+        value = value + swap(value, bit)
+    return value
+
+
+def sum_ring(value):
+    return value + shift(value, 1) + shift(value, 2) + shift(value, 3)
+
+
+def dot(left, right, dims=NN):
+    return lax.dot_general(left, right, dims, preferred_element_type=F32)
+
+
+def inverse_rms(values):
+    return lax.rsqrt(jnp.mean(values * values, axis=-1, keepdims=True) + EPSILON)
+
+
+CHIPS = (0, 1, 2, 3)
+
+
+def to_chips(value):
+    return [value] + [swap(value, 2 * mask) for mask in CHIPS[1:]]
 
 
 def local(
@@ -306,168 +533,141 @@
     downward_weight,
     cotangent,
 ):
-    shard_len, rows_here, model_width = tokens.shape
+    shard, rows_here, width = tokens.shape
     length = segment_ids.shape[1]
-    num_buckets, heads_here = rel_bias.shape
-    head_dim = w_query.shape[1] // heads_here
+    heads = rel_bias.shape[1]
+    feats = w_query.shape[1]
+    units = downward_weight.shape[0]
+    ring = lax.axis_size("tensor")
+    n_dp = lax.axis_size("dp")
+    z = lax.axis_index("tensor")
+    dp = lax.axis_index("dp")
+    core = dp & 1
+    chip = (dp >> 1) & 3
+    where = jnp.stack([core, chip, dp]).astype(jnp.int32)
+
+    x_low = tokens.reshape(shard, width)
+    cot = cotangent.reshape(shard, width)
     row_tiles, col_tiles = bias_tiles(rel_bias)
-    x_in = tokens.astype(jnp.float32)
-    norm_one = rms_norm(x_in, norm1_gain).astype(jnp.bfloat16)
-    full_one = lax.all_gather(norm_one, "tensor", axis=0, tiled=True)
-
-    def project(weight):
-        return jnp.einsum(
-            "trd,dc->rtc", full_one, weight, preferred_element_type=jnp.float32
-        ).astype(jnp.bfloat16)
-
-    q = project(w_query)
-    k = project(w_key)
-    v = project(w_value)
-    mixed, lse = attn_fwd(segment_ids, rel_bias, q[0], k[0], v[0], row_tiles)
-    mixed_flat = mixed[None]
-    portion = lax.slice_in_dim(mixed_flat, 0, shard_len * lax.axis_size("tensor"), axis=1)
-    attn_sum = lax.psum_scatter(
-        jnp.einsum("rtc,cd->trd", portion, w_out, preferred_element_type=jnp.float32).astype(
-            jnp.bfloat16
-        ),
-        "tensor",
-        scatter_dimension=0,
-        tiled=True,
-    ).astype(jnp.float32)
-    hidden_in = x_in + attn_sum
-    norm_two = rms_norm(hidden_in, norm2_gain).astype(jnp.bfloat16)
-    whole_second = lax.all_gather(norm_two, "tensor", axis=0, tiled=True)
-    gate_preactivation = jnp.einsum(
-        "hzo,on->hzn", whole_second, gate_weight_matrix, preferred_element_type=jnp.float32
+    w_qkv = jnp.concatenate([w_query, w_key, w_value], axis=1)
+
+    blocks = [x_low]
+    blocks.append(shift(blocks[-1], 1))
+    blocks.append(shift(blocks[-1], 1))
+    cs = to_chips(cot)
+    blocks.append(shift(after(blocks[-1], *cs), 1))
+    out_rows = feats // n_dp
+    out_piece = lax.dynamic_slice_in_dim(w_out, dp * out_rows, out_rows, 0)
+    out_ring = lax.all_to_all(jnp.broadcast_to(out_piece, (ring, *out_piece.shape)), "tensor", 0, 0, tiled=True)
+    out_ring = after(out_ring, *cs)
+    out_all = lax.all_to_all(jnp.broadcast_to(out_ring, (n_dp, *out_ring.shape)), "dp", 0, 0, tiled=True)
+    out_all = jnp.moveaxis(out_all, 0, 1).reshape(ring * feats, width)
+
+    def unit_rows(array):
+        return lax.dynamic_slice(array, (chip * (units // 4), core * (width // 2)), (units // 4, width // 2))
+
+    pack = jnp.concatenate(
+        [
+            unit_rows(jnp.transpose(gate_weight_matrix)),
+            unit_rows(jnp.transpose(upward_weight)),
+            unit_rows(downward_weight),
+        ],
+        axis=0,
     )
-    upward_preactivation = jnp.einsum(
-        "hzo,on->hzn", whole_second, upward_weight, preferred_element_type=jnp.float32
+    mine_w = lax.all_gather(after(pack, blocks[2]), "tensor", axis=0)
+    other_w = swap(mine_w, 1)
+
+    qkv = jnp.zeros((length, 3 * feats), BF16)
+    norm_full = jnp.zeros((length, width), BF16)
+    for s, block in enumerate(blocks):
+        values = block.astype(F32)
+        normed = (values * inverse_rms(values) * norm1_gain).astype(BF16)
+        start = ((z - s) % ring) * shard
+        norm_full = lax.dynamic_update_slice_in_dim(norm_full, normed, start, 0)
+        qkv = lax.dynamic_update_slice_in_dim(qkv, dot(normed, w_qkv).astype(BF16), start, 0)
+
+    o_row, lse = attn_fwd(segment_ids, rel_bias, qkv, row_tiles)
+    o_home = lax.all_to_all(o_row, "tensor", 0, 1, tiled=True)
+    attn = dot(o_home, out_all)
+    x_one = x_low.astype(F32) + attn
+    r_two = inverse_rms(x_one)
+    norm_two = (x_one * r_two * norm2_gain).astype(BF16)
+
+    xs = to_chips(norm_two)
+    parts = [ffn(where, x, c, mine_w, other_w) for x, c in zip(xs, cs)]
+
+    keep, give = ffn_grads(
+        where, [part[2] for part in parts], cs, [part[3] for part in parts], xs, [part[4] for part in parts], ring
     )
-    hidden_state = gelu_mix(gate_preactivation, upward_preactivation).astype(jnp.bfloat16)
-    portion = lax.slice_in_dim(hidden_state, 0, lax.axis_size("tensor") * shard_len, axis=0)
-    ffn_sum = lax.psum_scatter(
-        jnp.einsum(
-            "kwc,cn->kwn", portion, downward_weight, preferred_element_type=jnp.float32
-        ).astype(jnp.bfloat16),
-        "tensor",
-        scatter_dimension=0,
-        tiled=True,
-    ).astype(jnp.float32)
-    out_value = hidden_in + ffn_sum
-    out_tokens = out_value.astype(jnp.bfloat16)
-    stat_parts = jnp.stack(
-        [jnp.sum(attn_sum * attn_sum), jnp.sum(ffn_sum * ffn_sum), jnp.sum(out_value * out_value)]
+
+    def sum_chips(terms):
+        total = terms[0].astype(F32)
+        for mask in CHIPS[1:]:
+            total = total + swap(terms[mask], 2 * mask).astype(F32)
+        return total
+
+    d_two = sum_chips([after(parts[0][0], keep)] + [part[0] for part in parts[1:]])
+    u_two = d_two * norm2_gain
+    d_x_one = cot.astype(F32) + r_two * u_two - x_one * (
+        r_two * r_two * r_two * jnp.mean(u_two * x_one, axis=-1, keepdims=True)
     )
-    _, mix_back = jax.vjp(gelu_mix, gate_preactivation, upward_preactivation)
-    cotangent_whole = lax.all_gather(cotangent, "tensor", axis=0, tiled=True)
-    downward_weight_gradient = jnp.einsum(
-        "kpo,kpb->ob", hidden_state, cotangent_whole, preferred_element_type=jnp.float32
-    )
-    hidden_gradient = jnp.einsum(
-        "gqm,zm->gqz", cotangent_whole, downward_weight, preferred_element_type=jnp.float32
-    )
-    d_gate_f, d_up_f = mix_back(hidden_gradient)
-    gate_gradient = d_gate_f.astype(jnp.bfloat16)
-    upward_gradient = d_up_f.astype(jnp.bfloat16)
-    gate_weight_gradient = jnp.einsum(
-        "zyv,zya->va", whole_second, gate_gradient, preferred_element_type=jnp.float32
-    )
-    upward_weight_gradient = jnp.einsum(
-        "zyv,zya->va", whole_second, upward_gradient, preferred_element_type=jnp.float32
-    )
-    row_count = lax.axis_size("tensor") * shard_len
-    gate_portion = lax.slice_in_dim(gate_gradient, 0, row_count, axis=0)
-    upward_portion = lax.slice_in_dim(upward_gradient, 0, row_count, axis=0)
-    d_norm_two = lax.psum_scatter(
-        (
-            jnp.einsum(
-                "xas,ks->xak", gate_portion, gate_weight_matrix, preferred_element_type=jnp.float32
-            )
-            + jnp.einsum(
-                "xas,ks->xak", upward_portion, upward_weight, preferred_element_type=jnp.float32
-            )
-        ).astype(jnp.bfloat16),
-        "tensor",
-        scatter_dimension=0,
-        tiled=True,
-    ).astype(jnp.float32)
-    d_from_two, grad_two_part = norm_back(hidden_in, norm2_gain, d_norm_two)
-    d_hidden_in = cotangent.astype(jnp.float32) + d_from_two
-    d_attn = d_hidden_in.astype(jnp.bfloat16)
-    d_attn_full = lax.all_gather(d_attn, "tensor", axis=0, tiled=True)
-    grad_out = jnp.einsum(
-        "rtc,trd->cd", mixed_flat, d_attn_full, preferred_element_type=jnp.float32
-    )
-    d_mixed = jnp.einsum(
-        "trd,cd->rtc", d_attn_full, w_out, preferred_element_type=jnp.float32
-    ).astype(jnp.bfloat16)
-    dq, dk, dv, near, far = attn_bwd(
-        segment_ids, rel_bias, q[0], k[0], v[0], mixed, d_mixed[0], lse, col_tiles
-    )
-    grad_bias = bias_grad(near, far)[:, :heads_here]
-    dq_flat, dk_flat, dv_flat = dq[None], dk[None], dv[None]
-    grad_query = jnp.einsum("trd,rtc->dc", full_one, dq_flat, preferred_element_type=jnp.float32)
-    grad_key = jnp.einsum("trd,rtc->dc", full_one, dk_flat, preferred_element_type=jnp.float32)
-    grad_value = jnp.einsum("trd,rtc->dc", full_one, dv_flat, preferred_element_type=jnp.float32)
-    row_count = lax.axis_size("tensor") * shard_len
-    term_sum = jnp.einsum(
-        "rtc,dc->trd",
-        lax.slice_in_dim(dq_flat, 0, row_count, axis=1),
-        w_query,
-        preferred_element_type=jnp.float32,
-    )
-    term_sum = term_sum + jnp.einsum(
-        "rtc,dc->trd",
-        lax.slice_in_dim(dk_flat, 0, row_count, axis=1),
-        w_key,
-        preferred_element_type=jnp.float32,
-    )
-    d_norm_one = lax.psum_scatter(
-        (
-            term_sum
-            + jnp.einsum(
-                "rtc,dc->trd",
-                lax.slice_in_dim(dv_flat, 0, row_count, axis=1),
-                w_value,
-                preferred_element_type=jnp.float32,
-            )
-        ).astype(jnp.bfloat16),
-        "tensor",
-        scatter_dimension=0,
-        tiled=True,
-    ).astype(jnp.float32)
-    d_from_one, grad_one_part = norm_back(x_in, norm1_gain, d_norm_one)
-    grad_tokens = (d_hidden_in + d_from_one).astype(jnp.bfloat16)
-    big = (
-        grad_query,
-        grad_key,
-        grad_value,
-        grad_out,
-        gate_weight_gradient,
-        upward_weight_gradient,
-        downward_weight_gradient,
-    )
-    big = lax.psum(tuple(g.astype(jnp.bfloat16) for g in big), "dp")
-    (
-        grad_query,
-        grad_key,
-        grad_value,
-        grad_out,
-        gate_weight_gradient,
-        upward_weight_gradient,
-        downward_weight_gradient,
-    ) = (g.astype(jnp.float32) for g in big)
-    grad_bias = lax.psum(grad_bias, "dp")
-    grad_norm1, grad_norm2, stat_sums = lax.psum(
-        (grad_one_part, grad_two_part, stat_parts), ("dp", "tensor")
-    )
-    element_count = (
-        shard_len * rows_here * model_width * lax.axis_size("dp") * lax.axis_size("tensor")
-    )
-    rms_stats = jnp.sqrt(stat_sums / element_count)
+    d_attn = d_x_one.astype(BF16)
+    d_o = dot(d_attn, out_all, NT).astype(BF16)
+    do_row = lax.all_to_all(d_o, "tensor", 1, 0, tiled=True)
+    ffo = sum_chips([after(part[1], d_o) for part in parts])
+    y = x_one + ffo
+    out_tokens = y.astype(BF16)
+    grad_two = jnp.sum(d_two * x_one * r_two, axis=0)
+    stats = jnp.stack([jnp.sum(attn * attn), jnp.sum(ffo * ffo), jnp.sum(y * y)])
+
+    dqkv, near, far = attn_bwd(segment_ids, rel_bias, qkv, o_row, do_row, lse, col_tiles)
+    d_one_part = dot(dqkv, w_qkv, NT).astype(BF16)
+    d_one = lax.psum_scatter(d_one_part, "tensor", scatter_dimension=0, tiled=True).astype(F32)
+    x_in = x_low.astype(F32)
+    r_one = inverse_rms(x_in)
+    u_one = d_one * norm1_gain
+    grad_tokens = (
+        d_x_one + r_one * u_one - x_in * (r_one * r_one * r_one * jnp.mean(u_one * x_in, axis=-1, keepdims=True))
+    ).astype(BF16)
+
+    keep = add(keep, swap(give, 1))
+
+    def share_of(s):
+        return lax.dynamic_index_in_dim(keep, (z - s) % ring, 0, keepdims=False)
+
+    piece = after(share_of(1), d_o)
+    for s in (2, 3, 0):
+        piece = add(shift(piece, 1), share_of(s))
+    for bit in bits_from(8):
+        piece = add(piece, swap(piece, bit))
+    own = jnp.stack(to_chips(piece))
+    grad_gate, grad_up, grad_down = place(where, own, swap(own, 1), CHIPS)
+    grad_gate, grad_up = jnp.transpose(grad_gate), jnp.transpose(grad_up)
+
+    grad_o = dot(o_home, d_attn, TN).astype(BF16).reshape(ring, n_dp, out_rows, width)
+    got = lax.all_to_all(jnp.moveaxis(grad_o, 1, 0), "dp", 0, 0, tiled=True)
+    got = jnp.sum(got.astype(F32), axis=0).astype(BF16)
+    got = lax.all_to_all(got, "tensor", 0, 0, tiled=True)
+    pieces, masks = gather_all(jnp.sum(got.astype(F32), axis=0).astype(BF16))
+    (grad_out,) = place_rows(where, pieces, masks, 1)
+
+    grad_qkv = dot(norm_full, after(dqkv, d_one_part), TN)
+    grad_one = jnp.sum(grad_qkv * w_qkv.astype(F32), axis=1) / norm1_gain
+    got = lax.all_to_all(grad_qkv.astype(BF16).reshape(n_dp, width // n_dp, 3 * feats), "dp", 0, 0, tiled=True)
+    pieces, masks = gather_all(jnp.sum(got.astype(F32), axis=0).astype(BF16))
+    grad_query, grad_key, grad_value = place_rows(where, pieces, masks, 3)
+
+    small = jnp.concatenate([grad_two, stats, grad_one, bias_grad(near, far)[:, :heads].reshape(-1)])
+    small = sum_rows(small)
+    grad_bias = small[2 * width + 3 :].reshape(-1, heads)
+    small = sum_ring(small[: 2 * width + 3])
+    grad_norm2, stat_sums, grad_norm1 = small[:width], small[width : width + 3], small[width + 3 :]
+    count = shard * rows_here * width * n_dp * ring
+    rms_stats = jnp.sqrt(stat_sums / count)
+    shape = (shard, rows_here, width)
     return (
-        out_tokens,
-        grad_tokens,
+        out_tokens.reshape(shape),
+        grad_tokens.reshape(shape),
         grad_norm1,
         grad_query,
         grad_key,
@@ -475,9 +675,9 @@
         grad_out,
         grad_bias,
         grad_norm2,
-        gate_weight_gradient,
-        upward_weight_gradient,
-        downward_weight_gradient,
+        grad_gate,
+        grad_up,
+        grad_down,
         rms_stats,
     )
 

time: 651 us -> 452 us (0.69)
  waiting for transfers between devices: 422 us -> 193 us
  blocking collectives: 73.9 us -> 0 us
  starting transfers between devices: 10.6 us -> 76 us
  Pallas kernels: 25.2 us -> 74.1 us
  matrix products: 60.1 us -> 21.5 us
  local copies, waits for them, and re-layouts: 6.11 us -> 26.5 us
  other arithmetic: 29.9 us -> 38.3 us
    reduce_scatter x4 -> x1, waiting for transfers between devices: 184 us -> 0.01 us  [local(): lax.psum_scatter(d_one_part, 'tensor', scatter_dimension=0, tiled=True)]
    ppermute x0 -> x36, waiting for transfers between devices: none -> 152 us  [the longest x9 92 us: shift(): lax.ppermute(value, 'tensor', [(i, (i + step) % size) for i in range(size)])]
    all_gather x4 -> x1, waiting for transfers between devices: 166 us -> 29 us  [local(): mine_w = lax.all_gather(after(pack, blocks[2]), 'tensor', axis=0)]
    psum x2 -> x0, blocking collectives: 73.9 us -> none  [the longest x1 39.9 us: local(): lax.psum((grad_one_part, grad_two_part, stat_parts), ('dp', 'tensor'))]
    psum x1 -> x0, waiting for transfers between devices: 70.7 us -> none  [local(): big = lax.psum(tuple((g.astype(jnp.bfloat16) for g in big)), 'dp')]
    pallas_call x1 -> x9, Pallas kernels: 8.72 us -> 56.8 us  [the longest x4 25 us: ffn(): pl.pallas_call(ffn_kernel, out_shape=(wide, wide, inner, inner, inner), i...]
    ppermute x0 -> x36, starting transfers between devices: none -> 39.4 us  [the longest x27 29.2 us: swap(): return lax.ppermute(value, 'dp', [(i, i ^ mask) for i in range(size)])]
    dot_general x21 -> x9, matrix products: 60.1 us -> 21.5 us  [dot(): return lax.dot_general(left, right, dims, preferred_element_type=F32)]
  transfers between devices with their start and end apart: 9 -> 45, of which waited for: 9 -> 22; matrix products, arithmetic and copies ran while one was open for 7% -> 17% of each run, Pallas kernels for 1% -> 15%
where the time goes in v1:
time: 452 us; the launch traced here: 444 us
  waiting for transfers between devices  193 us (43%)
  starting transfers between devices  76 us (17%)
  Pallas kernels  74.1 us (16%)
  other arithmetic  38.3 us (8%)
  local copies, waits for them, and re-layouts  26.5 us (6%)
  matrix products  21.5 us (5%)
  between operations  15.2 us (3%)
    ppermute x9, waiting for transfers between devices, shift(): lax.ppermute(value, 'tensor', [(i, (i + step) % size) for i in range(size)])  92 us
    ppermute x27, waiting for transfers between devices, swap(): return lax.ppermute(value, 'dp', [(i, i ^ mask) for i in range(size)])  60.4 us
    ppermute x27, starting transfers between devices, swap(): return lax.ppermute(value, 'dp', [(i, i ^ mask) for i in range(size)])  29.2 us
    all_gather x1, waiting for transfers between devices, local(): mine_w = lax.all_gather(after(pack, blocks[2]), 'tensor', axis=0)  29 us
    pallas_call x4, Pallas kernels, ffn(): pl.pallas_call(ffn_kernel, out_shape=(wide, wide, inner, inner, inner), i...  25 us
    dot_general x9, matrix products, dot(): return lax.dot_general(left, right, dims, preferred_element_type=F32)  21.5 us
    pallas_call x1, Pallas kernels, ffn_grads(): pl.pallas_call(functools.partial(ffn_grads_kernel, n), out_shape=(shape,...  11.6 us
    all_to_all x1, starting transfers between devices, local(): lax.all_to_all(grad_qkv.astype(BF16).reshape(n_dp, width // n_dp, 3 * fea...  11.5 us
  transfers between devices with their start and end apart: 45, of which 22 were waited for; matrix products, arithmetic and copies ran while one was open for 17% of the time, Pallas kernels for 15%

profile of v1, /device:TPU:0, one launch (start us, length us, event | category | flops | bytes accessed | tf_op | source)
XLA Modules:
  0.0 444.2 jit_solution(2133465884249105486)
XLA Ops:
  7.2 3.0 collective-permute-start.2
  14.6 3.9 all-to-all-start.1
  22.4 5.2 %bias_tiles.1 = (f32[4,3,128,128]{3,2,1,0:T(8,128)}, f32[4,3,128,128]{3,2,1,0:T(8,128)}) custom-call(f32[32,4]{1,0:T(8,128)} %copy.46.bias_ref), custom_call_target="tpu_custom_call" | custom-call | tf_op jit(solution)/shard_map/bias_tiles/pallas_call | solution.py:48
  31.4 2.7 all-to-all-done.1
  34.1 3.7 collective-permute-done.3.c_ref.refs_6_
  39.5 4.4 all-to-all-start.2
  49.1 12.5 %collective-permute-done.1 = bf16[288,1024]{1,0:T(8,128)(2,1)S(1)} collective-permute-done((bf16[288,1024]{1,0:T(8,128)(2,1)}, bf16[288,1024]{1,0:T(8,128)(2,1)S(1)}, u32[]{:S(2)}, u32[]{:S(2)}) %collective-permute-start.1) | collective-permute-done | bytes 589856 | tf_op jit(solution)/shard_map/ppermute | solution.py:470
  64.3 18.1 %collective-permute-done.5 = bf16[288,1024]{1,0:T(8,128)(2,1)S(1)} collective-permute-done((bf16[288,1024]{1,0:T(8,128)(2,1)S(1)}, bf16[288,1024]{1,0:T(8,128)(2,1)S(1)}, u32[]{:S(2)}, u32[]{:S(2)}) %collective-permute-start.5) | collective-permute-done | bytes 589856 | tf_op jit(solution)/shard_map/ppermute | solution.py:470
  83.8 8.5 %attn_fwd.1 = (bf16[1152,256]{1,0:T(8,128)(2,1)}, f32[4,8,1152]{2,1,0:T(8,128)S(1)}) custom-call(s32[1,1152]{1,0:T(1,128)S(1)} %copy-done.20, f32[32,4]{1,0:T(8,128)S(1)} %copy-done.6, bf16[1152,768]{1,0:T(8,128)(2,1)S(1)} %fusion.qkv_ref, f32[4,3,128,128]{3,2,1,0:T(8,128)S(1)} %copy-done.12), custom_call_target="tpu_custom_call" | custom-call | flops 20000000000 | bytes 4000000 | tf_op jit(solution)/shard_map/attn_fwd/pallas_call | solution.py:150
  92.3 4.7 %all-to-all-start = ((bf16[4,288,256]{2,1,0:T(8,128)(2,1)}), bf16[4,288,256]{2,1,0:T(8,128)(2,1)}, u32[]{:S(2)}, u32[]{:S(2)}) async-start(bf16[4,288,256]{2,1,0:T(8,128)(2,1)} %bitcast.2), calls=%async_computation | async-start | bytes 1179648 | tf_op jit(solution)/shard_map/all_to_all | solution.py:590
  96.9 29.0 %all-gather.3.cloned.1.call-done = bf16[2112,512]{1,0:T(8,128)(2,1)} async-done(((bf16[528,512]{1,0:T(8,128)(2,1)}), bf16[2112,512]{1,0:T(8,128)(2,1)}) %all-gather.3.cloned.1.call-update) | async-done | bytes 2162704 | tf_op jit(solution)/shard_map/all_gather | solution.py:577
  125.9 3.2 copy.48
  130.4 3.3 multiply_reduce_fusion.6
  133.9 3.0 collective-permute-start.9
  137.7 13.5 %collective-permute-done.9.x_ref.refs_15_ = bf16[288,1024]{1,0:T(8,128)(2,1)S(1)} collective-permute-done((bf16[288,1024]{1,0:T(8,128)(2,1)S(1)}, bf16[288,1024]{1,0:T(8,128)(2,1)S(1)}, u32[]{:S(2)}, u32[]{:S(2)}) %collective-permute-start.9) | collective-permute-done | bytes 589856 | tf_op jit(solution)/shard_map/ppermute | solution.py:465
  151.2 7.0 %ffn.7 = (bf16[288,1024]{1,0:T(8,128)(2,1)S(1)}, bf16[288,1024]{1,0:T(8,128)(2,1)}, bf16[288,704]{1,0:T(8,128)(2,1)S(1)}, bf16[288,704]{1,0:T(8,128)(2,1)S(1)}, bf16[288,704]{1,0:T(8,128)(2,1)S(1)}) custom-call(s32[3]{0:T(128)S(1)} %pad_add_fusion.where_ref, bf16[288,1024]{1,0:T(8,128)(2,1)S(1)} %collective-permute-done.9.x_ref.refs_15_, ...), custom_call_target="tpu_custom_call" | custom-call | flops 3321888768 | bytes 7274496 | tf_op jit(solution)/shard_map/ffn/pallas_call | solution.py:344
  158.2 2.9 collective-permute-start.12
  161.1 2.6 collective-permute-done.8.x_ref.refs_14_
  163.7 6.2 %ffn.6 = (bf16[288,1024]{1,0:T(8,128)(2,1)S(1)}, bf16[288,1024]{1,0:T(8,128)(2,1)}, bf16[288,704]{1,0:T(8,128)(2,1)S(1)}, bf16[288,704]{1,0:T(8,128)(2,1)S(1)}, bf16[288,704]{1,0:T(8,128)(2,1)S(1)}) custom-call(s32[3]{0:T(128)S(1)} %pad_add_fusion.where_ref, bf16[288,1024]{1,0:T(8,128)(2,1)S(1)} %collective-permute-done.8.x_ref.refs_14_, ...), custom_call_target="tpu_custom_call" | custom-call | flops 3321888768 | bytes 7274496 | tf_op jit(solution)/shard_map/ffn/pallas_call | solution.py:344
  170.1 6.4 %ffn.5 = (bf16[288,1024]{1,0:T(8,128)(2,1)S(1)}, bf16[288,1024]{1,0:T(8,128)(2,1)}, bf16[288,704]{1,0:T(8,128)(2,1)S(1)}, bf16[288,704]{1,0:T(8,128)(2,1)S(1)}, bf16[288,704]{1,0:T(8,128)(2,1)S(1)}) custom-call(s32[3]{0:T(128)S(1)} %pad_add_fusion.where_ref, bf16[288,1024]{1,0:T(8,128)(2,1)S(1)} %collective-permute-done.7.x_ref.refs_13_, ...), custom_call_target="tpu_custom_call" | custom-call | flops 3321888768 | bytes 7274496 | tf_op jit(solution)/shard_map/ffn/pallas_call | solution.py:344
  178.7 5.4 %ffn.4 = (bf16[288,1024]{1,0:T(8,128)(2,1)S(1)}, bf16[288,1024]{1,0:T(8,128)(2,1)S(1)}, bf16[288,704]{1,0:T(8,128)(2,1)S(1)}, bf16[288,704]{1,0:T(8,128)(2,1)S(1)}, bf16[288,704]{1,0:T(8,128)(2,1)S(1)}) custom-call(s32[3]{0:T(128)S(1)} %pad_add_fusion.where_ref, bf16[288,1024]{1,0:T(8,128)(2,1)S(1)} %multiply_convert_fusion.x_ref.refs_12_, ...), custom_call_target="tpu_custom_call" | custom-call | flops 3321888768 | bytes 7274496 | tf_op jit(solution)/shard_map/ffn/pallas_call | solution.py:344
  184.1 11.6 %ffn_grads.1 = (bf16[4,3,176,512]{3,2,1,0:T(8,128)(2,1)}, bf16[4,3,176,512]{3,2,1,0:T(8,128)(2,1)}) custom-call(s32[3]{0:T(128)S(1)} %pad_add_fusion.where_ref, bf16[288,704]{1,0:T(8,128)(2,1)S(1)} %get-tuple-element.65.refs_0_, bf16[288,704]{1,0:T(8,128)(2,1)S(1)} %get-tuple-element.66.refs_1_, bf16[288,704]{1,0:T(8,128)(2,1)S(1)} %get-tuple-element.67.refs_2_, ...), custom_call_target="tpu_custom_call" | custom-call | flops 4982833152 | bytes 9584640 | tf_op jit(solution)/shard_map/ffn_grads/pallas_call | solution.py:400
  199.9 3.7 all-to-all-start.3
  210.5 8.5 %all-to-all-done.3 = bf16[288,4,256]{2,0,1:T(8,128)(2,1)S(1)} async-done(((bf16[288,4,256]{2,0,1:T(8,128)(2,1)}), bf16[288,4,256]{2,0,1:T(8,128)(2,1)S(1)}, u32[]{:S(2)}, u32[]{:S(2)}) %all-to-all-start.3) | async-done | bytes 589856 | tf_op jit(solution)/shard_map/all_to_all | solution.py:616
  219.0 9.1 %attn_bwd.1 = (bf16[1152,768]{1,0:T(8,128)(2,1)S(1)}, f32[4,3,128,128]{3,2,1,0:T(8,128)S(1)}, f32[4,2,8,128]{3,2,1,0:T(8,128)S(1)}) custom-call(s32[1,1152]{1,0:T(1,128)S(1)} %copy-done.20, f32[32,4]{1,0:T(8,128)S(1)} %copy-done.6, bf16[1152,768]{1,0:T(8,128)(2,1)} %copy-done.2, bf16[1152,256]{1,0:T(8,128)(2,1)} %get-tuple-element.60.o_ref, ...), custom_call_target="tpu_custom_call" | custom-call | flops 40000000000 | bytes 6000000 | tf_op jit(solution)/shard_map/attn_bwd/pallas_call | solution.py:255
  230.8 3.4 convolution_convert_fusion
  234.3 5.7 %fusion.37 = (bf16[1024,768]{1,0:T(8,128)(2,1)}, f32[1024]{0:T(1024)S(1)}) fusion(bf16[1024,768]{1,0:T(8,128)(2,1)S(1)} %copy-done.48, bf16[1152,1024]{1,0:T(8,128)(2,1)} %fusion.27, bf16[1152,768]{1,0:T(8,128)(2,1)} %copy-done.21), kind=kOutput, calls=%fused_computation.95 | convolution fusion | flops 1815084032 | bytes 7278592 | tf_op jit(solution)/shard_map/dot_general | solution.py:507
  240.0 11.5 %all-to-all-start.4 = ((bf16[8,128,768]{2,1,0:T(8,128)(2,1)}), bf16[8,128,768]{2,1,0:T(8,128)(2,1)}, u32[]{:S(2)}, u32[]{:S(2)}) async-start(bf16[8,128,768]{2,1,0:T(8,128)(2,1)} %bitcast.20), calls=%async_computation.5 | async-start | bytes 3145728 | tf_op jit(solution)/shard_map/all_to_all | solution.py:656
  251.6 2.9 add_convert_fusion
  255.4 21.3 %collective-permute-done.29 = bf16[3,176,512]{2,1,0:T(8,128)(2,1)} collective-permute-done((bf16[3,176,512]{2,1,0:T(8,128)(2,1)}, bf16[3,176,512]{2,1,0:T(8,128)(2,1)}, u32[]{:S(2)}, u32[]{:S(2)}) %collective-permute-start.29) | collective-permute-done | bytes 540704 | tf_op jit(solution)/shard_map/ppermute | solution.py:470
  282.8 5.0 %all-to-all-start.5 = ((bf16[8,4,32,1024]{3,2,1,0:T(8,128)(2,1)}), bf16[8,4,32,1024]{3,2,1,0:T(8,128)(2,1)}, u32[]{:S(2)}, u32[]{:S(2)}) async-start(bf16[8,4,32,1024]{3,2,1,0:T(8,128)(2,1)} %bitcast.92), calls=%async_computation.6 | async-start | bytes 4194304 | tf_op jit(solution)/shard_map/all_to_all | solution.py:648
  287.9 19.9 %collective-permute-done.30 = bf16[3,176,512]{2,1,0:T(8,128)(2,1)} collective-permute-done((bf16[3,176,512]{2,1,0:T(8,128)(2,1)}, bf16[3,176,512]{2,1,0:T(8,128)(2,1)}, u32[]{:S(2)}, u32[]{:S(2)}) %collective-permute-start.30) | collective-permute-done | bytes 540704 | tf_op jit(solution)/shard_map/ppermute | solution.py:470
  309.7 4.0 collective-permute-start.31
  313.7 20.3 %collective-permute-done.31 = bf16[3,176,512]{2,1,0:T(8,128)(2,1)} collective-permute-done((bf16[3,176,512]{2,1,0:T(8,128)(2,1)}, bf16[3,176,512]{2,1,0:T(8,128)(2,1)}, u32[]{:S(2)}, u32[]{:S(2)}) %collective-permute-start.31) | collective-permute-done | bytes 540704 | tf_op jit(solution)/shard_map/ppermute | solution.py:470
  342.2 2.7 reduce_sum.161
  344.9 3.4 all-to-all-start.6
  349.8 6.2 %collective-permute-done.22 = bf16[1,128,768]{2,1,0:T(8,128)(2,1)S(1)} collective-permute-done((bf16[1,128,768]{2,1,0:T(8,128)(2,1)S(1)}, bf16[1,128,768]{2,1,0:T(8,128)(2,1)S(1)}, u32[]{:S(2)}, u32[]{:S(2)}) %collective-permute-start.22) | collective-permute-done | bytes 196640 | tf_op jit(solution)/shard_map/ppermute | solution.py:465
  358.9 3.0 collective-permute-done.33
  361.9 5.7 %collective-permute-done.32 = bf16[3,176,512]{2,1,0:T(8,128)(2,1)S(1)} collective-permute-done((bf16[3,176,512]{2,1,0:T(8,128)(2,1)}, bf16[3,176,512]{2,1,0:T(8,128)(2,1)S(1)}, u32[]{:S(2)}, u32[]{:S(2)}) %collective-permute-start.32) | collective-permute-done | bytes 540704 | tf_op jit(solution)/shard_map/ppermute | solution.py:465
  370.6 10.3 %collective-permute-done.15 = bf16[288,1024]{1,0:T(8,128)(2,1)} collective-permute-done((bf16[288,1024]{1,0:T(8,128)(2,1)}, bf16[288,1024]{1,0:T(8,128)(2,1)}, u32[]{:S(2)}, u32[]{:S(2)}) %collective-permute-start.15) | collective-permute-done | bytes 589856 | tf_op jit(solution)/shard_map/ppermute | solution.py:465
  380.9 6.4 %collective-permute-done.14 = bf16[288,1024]{1,0:T(8,128)(2,1)} collective-permute-done((bf16[288,1024]{1,0:T(8,128)(2,1)}, bf16[288,1024]{1,0:T(8,128)(2,1)}, u32[]{:S(2)}, u32[]{:S(2)}) %collective-permute-start.14) | collective-permute-done | bytes 589856 | tf_op jit(solution)/shard_map/ppermute | solution.py:465
  387.3 3.0 collective-permute-done.13
  390.4 3.3 multiply_reduce_fusion.1
  393.7 3.6 bias_grad.1
  401.4 2.5 collective-permute-start.17
  421.7 2.5 pad_maximum_fusion.1.pieces_ref
  424.3 3.3 place_rows.2
  431.4 5.6 %place.1 = (f32[704,1024]{1,0:T(8,128)}, f32[704,1024]{1,0:T(8,128)}, f32[704,1024]{1,0:T(8,128)}) custom-call(s32[3]{0:T(128)S(1)} %copy-done.9, bf16[4,3,176,512]{3,2,1,0:T(8,128)(2,1)S(1)} %pad_maximum_fusion.own_ref, bf16[4,3,176,512]{3,2,1,0:T(8,128)(2,1)} %collective-permute-done.35.other_ref), custom_call_target="tpu_custom_call" | custom-call | bytes 25952256 | tf_op jit(solution)/shard_map/place/pallas_call | solution.py:429
  (233 shorter events, 91.2 us)
Async XLA Ops:
  7.2 26.9 %collective-permute-start.2 = (bf16[288,1024]{1,0:T(8,128)(2,1)}, bf16[288,1024]{1,0:T(8,128)(2,1)S(1)}, u32[]{:S(2)}, u32[]{:S(2)}) collective-permute-start(bf16[288,1024]{1,0:T(8,128)(2,1)} %bitcast.81), channel_id=1, source_target_pairs={{0,8},{4,12},{8,0},{12,4},{16,24},{20,28},{24,16},{28,20},{1,9},{5... | collective-permute-start | bytes 1769480 | tf_op jit(solution)/shard_map/ppermute | solution.py:465
  10.2 27.6 %collective-permute-start.3 = (bf16[288,1024]{1,0:T(8,128)(2,1)}, bf16[288,1024]{1,0:T(8,128)(2,1)S(1)}, u32[]{:S(2)}, u32[]{:S(2)}) collective-permute-start(bf16[288,1024]{1,0:T(8,128)(2,1)} %bitcast.82), channel_id=1, source_target_pairs={{0,16},{4,20},{8,24},{12,28},{16,0},{20,4},{24,8},{28,12},{1,17},{... | collective-permute-start | bytes 1769480 | tf_op jit(solution)/shard_map/ppermute | solution.py:465
  11.7 26.1 %collective-permute-start.4 = (bf16[288,1024]{1,0:T(8,128)(2,1)}, bf16[288,1024]{1,0:T(8,128)(2,1)}, u32[]{:S(2)}, u32[]{:S(2)}) collective-permute-start(bf16[288,1024]{1,0:T(8,128)(2,1)} %bitcast.83), channel_id=1, source_target_pairs={{0,24},{4,28},{8,16},{12,20},{16,8},{20,12},{24,0},{28,4},{1,25},{... | collective-permute-start | bytes 1769480 | tf_op jit(solution)/shard_map/ppermute | solution.py:465
  11.8 32.1 %collective-permute-start = (bf16[288,1024]{1,0:T(8,128)(2,1)}, bf16[288,1024]{1,0:T(8,128)(2,1)}, u32[]{:S(2)}, u32[]{:S(2)}) collective-permute-start(bf16[288,1024]{1,0:T(8,128)(2,1)} %bitcast.91), channel_id=1, source_target_pairs={{0,1},{1,2},{2,3},{3,0},{4,5},{5,6},{6,7},{7,4},{8,9},{9,10},{10,1... | collective-permute-start | bytes 1769480 | tf_op jit(solution)/shard_map/ppermute | solution.py:470
  14.6 19.6 %all-to-all-start.1 = ((bf16[4,32,1024]{2,1,0:T(8,128)(2,1)}), bf16[4,32,1024]{2,1,0:T(8,128)(2,1)S(1)}, u32[]{:S(2)}, u32[]{:S(2)}) async-start(bf16[4,32,1024]{2,1,0:T(8,128)(2,1)} %broadcast_in_dim.13), calls=%async_computation.1 | async-start | bytes 524288 | tf_op jit(solution)/shard_map/all_to_all | solution.py:561
  39.5 52.8 %all-to-all-start.2 = ((bf16[8,4,32,1024]{3,2,1,0:T(8,128)(2,1)}), bf16[8,4,32,1024]{3,2,1,0:T(8,128)(2,1)}, u32[]{:S(2)}, u32[]{:S(2)}) async-start(bf16[8,4,32,1024]{3,2,1,0:T(8,128)(2,1)} %broadcast_in_dim.14), calls=%async_computation.2 | async-start | bytes 4194304 | tf_op jit(solution)/shard_map/all_to_all | solution.py:563
  43.8 82.1 %all-gather.3.cloned.1.call-start = ((), (), s32[]{:S(2)}) async-start(), calls=%async_computation.9 | async-start | bytes 2703360 | tf_op jit(solution)/shard_map/all_gather | solution.py:577
  43.9 17.7 %collective-permute-start.1 = (bf16[288,1024]{1,0:T(8,128)(2,1)}, bf16[288,1024]{1,0:T(8,128)(2,1)S(1)}, u32[]{:S(2)}, u32[]{:S(2)}) collective-permute-start(bf16[288,1024]{1,0:T(8,128)(2,1)} %collective-permute-done), channel_id=1, source_target_pairs={{0,1},{1,2},{2,3},{3,0},{4,5},{5,6},{6,7},{7,4},{8,9},{9,10},{10,1... | collective-permute-start | bytes 1769480 | tf_op jit(solution)/shard_map/ppermute | solution.py:470
  61.6 20.8 %collective-permute-start.5 = (bf16[288,1024]{1,0:T(8,128)(2,1)S(1)}, bf16[288,1024]{1,0:T(8,128)(2,1)S(1)}, u32[]{:S(2)}, u32[]{:S(2)}) collective-permute-start(bf16[288,1024]{1,0:T(8,128)(2,1)S(1)} %collective-permute-done.1), channel_id=1, source_target_pairs={{0,1},{1,2},{2,3},{3,0},{4,5},{5,6},{6,7},{7,4},{8,9},{9,10},{10,1... | collective-permute-start | bytes 1769480 | tf_op jit(solution)/shard_map/ppermute | solution.py:470
  92.3 36.9 %all-to-all-start = ((bf16[4,288,256]{2,1,0:T(8,128)(2,1)}), bf16[4,288,256]{2,1,0:T(8,128)(2,1)}, u32[]{:S(2)}, u32[]{:S(2)}) async-start(bf16[4,288,256]{2,1,0:T(8,128)(2,1)} %bitcast.2), calls=%async_computation | async-start | bytes 1179648 | tf_op jit(solution)/shard_map/all_to_all | solution.py:590
  125.9 25.2 %collective-permute-start.6 = (bf16[4,528,512]{2,1,0:T(8,128)(2,1)}, bf16[4,528,512]{2,1,0:T(8,128)(2,1)S(1)}, u32[]{:S(2)}, u32[]{:S(2)}) collective-permute-start(bf16[4,528,512]{2,1,0:T(8,128)(2,1)} %bitcast.86), channel_id=1, source_target_pairs={{0,4},{4,0},{8,12},{12,8},{16,20},{20,16},{24,28},{28,24},{1,5},{5... | collective-permute-start | bytes 6488072 | tf_op jit(solution)/shard_map/ppermute | solution.py:465
  133.7 62.7 %copy-start.22 = (f32[288,1024]{1,0:T(8,128)}, f32[288,1024]{1,0:T(8,128)S(1)}, u32[]{:S(2)}) copy-start(f32[288,1024]{1,0:T(8,128)S(1)} %get-tuple-element.160) | copy-start | bytes 3538948
  133.9 44.8 %copy-start.5 = (bf16[288,1024]{1,0:T(8,128)(2,1)}, bf16[288,1024]{1,0:T(8,128)(2,1)S(1)}, u32[]{:S(2)}) copy-start(bf16[288,1024]{1,0:T(8,128)(2,1)S(1)} %multiply_convert_fusion.x_ref.refs_12_) | copy-start | bytes 1769476
  133.9 17.2 %collective-permute-start.9 = (bf16[288,1024]{1,0:T(8,128)(2,1)S(1)}, bf16[288,1024]{1,0:T(8,128)(2,1)S(1)}, u32[]{:S(2)}, u32[]{:S(2)}) collective-permute-start(bf16[288,1024]{1,0:T(8,128)(2,1)S(1)} %multiply_convert_fusion.x_ref.refs_12_), channel_id=1, source_target_pairs={{0,24},{4,28},{8,16},{12,20},{16,8},{20,12},{24,0},{28,4},{1,25},{... | collective-permute-start | bytes 1769480 | tf_op jit(solution)/shard_map/ppermute | solution.py:465
  136.9 26.8 %collective-permute-start.8 = (bf16[288,1024]{1,0:T(8,128)(2,1)S(1)}, bf16[288,1024]{1,0:T(8,128)(2,1)S(1)}, u32[]{:S(2)}, u32[]{:S(2)}) collective-permute-start(bf16[288,1024]{1,0:T(8,128)(2,1)S(1)} %multiply_convert_fusion.x_ref.refs_12_), channel_id=1, source_target_pairs={{0,16},{4,20},{8,24},{12,28},{16,0},{20,4},{24,8},{28,12},{1,17},{... | collective-permute-start | bytes 1769480 | tf_op jit(solution)/shard_map/ppermute | solution.py:465
  137.0 47.1 %copy-start.8 = (s32[3]{0:T(128)}, s32[3]{0:T(128)S(1)}, u32[]{:S(2)}) copy-start(s32[3]{0:T(128)S(1)} %pad_add_fusion.where_ref) | copy-start | bytes 40
  137.0 33.0 %collective-permute-start.7 = (bf16[288,1024]{1,0:T(8,128)(2,1)S(1)}, bf16[288,1024]{1,0:T(8,128)(2,1)S(1)}, u32[]{:S(2)}, u32[]{:S(2)}) collective-permute-start(bf16[288,1024]{1,0:T(8,128)(2,1)S(1)} %multiply_convert_fusion.x_ref.refs_12_), channel_id=1, source_target_pairs={{0,8},{4,12},{8,0},{12,4},{16,24},{20,28},{24,16},{28,20},{1,9},{5... | collective-permute-start | bytes 1769480 | tf_op jit(solution)/shard_map/ppermute | solution.py:465
  158.2 37.6 %collective-permute-start.12 = (bf16[288,1024]{1,0:T(8,128)(2,1)S(1)}, bf16[288,1024]{1,0:T(8,128)(2,1)S(1)}, u32[]{:S(2)}, u32[]{:S(2)}) collective-permute-start(bf16[288,1024]{1,0:T(8,128)(2,1)S(1)} %get-tuple-element.81), channel_id=1, source_target_pairs={{0,24},{4,28},{8,16},{12,20},{16,8},{20,12},{24,0},{28,4},{1,25},{... | collective-permute-start | bytes 1769480 | tf_op jit(solution)/shard_map/ppermute | solution.py:465
  170.0 25.8 %collective-permute-start.11 = (bf16[288,1024]{1,0:T(8,128)(2,1)S(1)}, bf16[288,1024]{1,0:T(8,128)(2,1)S(1)}, u32[]{:S(2)}, u32[]{:S(2)}) collective-permute-start(bf16[288,1024]{1,0:T(8,128)(2,1)S(1)} %get-tuple-element.80), channel_id=1, source_target_pairs={{0,16},{4,20},{8,24},{12,28},{16,0},{20,4},{24,8},{28,12},{1,17},{... | collective-permute-start | bytes 1769480 | tf_op jit(solution)/shard_map/ppermute | solution.py:465
  176.5 19.3 %collective-permute-start.10 = (bf16[288,1024]{1,0:T(8,128)(2,1)S(1)}, bf16[288,1024]{1,0:T(8,128)(2,1)S(1)}, u32[]{:S(2)}, u32[]{:S(2)}) collective-permute-start(bf16[288,1024]{1,0:T(8,128)(2,1)S(1)} %get-tuple-element.79), channel_id=1, source_target_pairs={{0,8},{4,12},{8,0},{12,4},{16,24},{20,28},{24,16},{28,20},{1,9},{5... | collective-permute-start | bytes 1769480 | tf_op jit(solution)/shard_map/ppermute | solution.py:465
  199.9 19.1 %all-to-all-start.3 = ((bf16[288,4,256]{2,0,1:T(8,128)(2,1)}), bf16[288,4,256]{2,0,1:T(8,128)(2,1)S(1)}, u32[]{:S(2)}, u32[]{:S(2)}) async-start(bf16[288,4,256]{2,0,1:T(8,128)(2,1)} %bitcast.77), calls=%async_computation.3 | async-start | bytes 1179648 | tf_op jit(solution)/shard_map/all_to_all | solution.py:616
  210.5 41.1 %collective-permute-start.28 = (bf16[4,3,176,512]{3,2,1,0:T(8,128)(2,1)}, bf16[4,3,176,512]{3,2,1,0:T(8,128)(2,1)}, u32[]{:S(2)}, u32[]{:S(2)}) collective-permute-start(bf16[4,3,176,512]{3,2,1,0:T(8,128)(2,1)} %get-tuple-element.98), channel_id=1, source_target_pairs={{0,4},{4,0},{8,12},{12,8},{16,20},{20,16},{24,28},{28,24},{1,5},{5... | collective-permute-start | bytes 6488072 | tf_op jit(solution)/shard_map/ppermute | solution.py:465
  240.0 42.8 %all-to-all-start.4 = ((bf16[8,128,768]{2,1,0:T(8,128)(2,1)}), bf16[8,128,768]{2,1,0:T(8,128)(2,1)}, u32[]{:S(2)}, u32[]{:S(2)}) async-start(bf16[8,128,768]{2,1,0:T(8,128)(2,1)} %bitcast.20), calls=%async_computation.5 | async-start | bytes 3145728 | tf_op jit(solution)/shard_map/all_to_all | solution.py:656
  251.5 176.1 %reduce-scatter.2.cloned.1.call-start = ((), (), s32[]{:S(2)}) async-start(), calls=%async_computation.8 | async-start | bytes 2949120 | tf_op jit(solution)/shard_map/reduce_scatter | solution.py:625
  255.3 21.4 %collective-permute-start.29 = (bf16[3,176,512]{2,1,0:T(8,128)(2,1)}, bf16[3,176,512]{2,1,0:T(8,128)(2,1)}, u32[]{:S(2)}, u32[]{:S(2)}) collective-permute-start(bf16[3,176,512]{2,1,0:T(8,128)(2,1)} %dynamic-slice_bitcast_fusion), channel_id=1, source_target_pairs={{0,1},{1,2},{2,3},{3,0},{4,5},{5,6},{6,7},{7,4},{8,9},{9,10},{10,1... | collective-permute-start | bytes 1622024 | tf_op jit(solution)/shard_map/ppermute | solution.py:470
  278.7 29.0 %collective-permute-start.30 = (bf16[3,176,512]{2,1,0:T(8,128)(2,1)}, bf16[3,176,512]{2,1,0:T(8,128)(2,1)}, u32[]{:S(2)}, u32[]{:S(2)}) collective-permute-start(bf16[3,176,512]{2,1,0:T(8,128)(2,1)} %fusion.21), channel_id=1, source_target_pairs={{0,1},{1,2},{2,3},{3,0},{4,5},{5,6},{6,7},{7,4},{8,9},{9,10},{10,1... | collective-permute-start | bytes 1622024 | tf_op jit(solution)/shard_map/ppermute | solution.py:470
  282.8 59.3 %all-to-all-start.5 = ((bf16[8,4,32,1024]{3,2,1,0:T(8,128)(2,1)}), bf16[8,4,32,1024]{3,2,1,0:T(8,128)(2,1)}, u32[]{:S(2)}, u32[]{:S(2)}) async-start(bf16[8,4,32,1024]{3,2,1,0:T(8,128)(2,1)} %bitcast.92), calls=%async_computation.6 | async-start | bytes 4194304 | tf_op jit(solution)/shard_map/all_to_all | solution.py:648
  309.7 24.3 %collective-permute-start.31 = (bf16[3,176,512]{2,1,0:T(8,128)(2,1)}, bf16[3,176,512]{2,1,0:T(8,128)(2,1)}, u32[]{:S(2)}, u32[]{:S(2)}) collective-permute-start(bf16[3,176,512]{2,1,0:T(8,128)(2,1)} %fusion.20), channel_id=1, source_target_pairs={{0,1},{1,2},{2,3},{3,0},{4,5},{5,6},{6,7},{7,4},{8,9},{9,10},{10,1... | collective-permute-start | bytes 1622024 | tf_op jit(solution)/shard_map/ppermute | solution.py:470
  336.0 21.1 %collective-permute-start.34 = (bf16[3,176,512]{2,1,0:T(8,128)(2,1)}, bf16[3,176,512]{2,1,0:T(8,128)(2,1)S(1)}, u32[]{:S(2)}, u32[]{:S(2)}) collective-permute-start(bf16[3,176,512]{2,1,0:T(8,128)(2,1)} %fusion.19), channel_id=1, source_target_pairs={{0,24},{4,28},{8,16},{12,20},{16,8},{20,12},{24,0},{28,4},{1,25},{... | collective-permute-start | bytes 1622024 | tf_op jit(solution)/shard_map/ppermute | solution.py:465
  339.6 16.4 %collective-permute-start.22 = (bf16[1,128,768]{2,1,0:T(8,128)(2,1)S(1)}, bf16[1,128,768]{2,1,0:T(8,128)(2,1)S(1)}, u32[]{:S(2)}, u32[]{:S(2)}) collective-permute-start(bf16[1,128,768]{2,1,0:T(8,128)(2,1)S(1)} %bitcast.93), channel_id=1, source_target_pairs={{0,8},{4,12},{8,0},{12,4},{16,24},{20,28},{24,16},{28,20},{1,9},{5... | collective-permute-start | bytes 589832 | tf_op jit(solution)/shard_map/ppermute | solution.py:465
  340.1 21.8 %collective-permute-start.33 = (bf16[3,176,512]{2,1,0:T(8,128)(2,1)}, bf16[3,176,512]{2,1,0:T(8,128)(2,1)S(1)}, u32[]{:S(2)}, u32[]{:S(2)}) collective-permute-start(bf16[3,176,512]{2,1,0:T(8,128)(2,1)} %fusion.19), channel_id=1, source_target_pairs={{0,16},{4,20},{8,24},{12,28},{16,0},{20,4},{24,8},{28,12},{1,17},{... | collective-permute-start | bytes 1622024 | tf_op jit(solution)/shard_map/ppermute | solution.py:465
  341.2 26.5 %collective-permute-start.32 = (bf16[3,176,512]{2,1,0:T(8,128)(2,1)}, bf16[3,176,512]{2,1,0:T(8,128)(2,1)S(1)}, u32[]{:S(2)}, u32[]{:S(2)}) collective-permute-start(bf16[3,176,512]{2,1,0:T(8,128)(2,1)} %fusion.19), channel_id=1, source_target_pairs={{0,8},{4,12},{8,0},{12,4},{16,24},{20,28},{24,16},{28,20},{1,9},{5... | collective-permute-start | bytes 1622024 | tf_op jit(solution)/shard_map/ppermute | solution.py:465
  344.9 13.2 %all-to-all-start.6 = ((bf16[4,32,1024]{2,1,0:T(8,128)(2,1)}), bf16[4,32,1024]{2,1,0:T(8,128)(2,1)S(1)}, u32[]{:S(2)}, u32[]{:S(2)}) async-start(bf16[4,32,1024]{2,1,0:T(8,128)(2,1)} %reduce_sum.161), calls=%async_computation.7 | async-start | bytes 524288 | tf_op jit(solution)/shard_map/all_to_all | solution.py:650
  348.3 32.6 %collective-permute-start.15 = (bf16[288,1024]{1,0:T(8,128)(2,1)}, bf16[288,1024]{1,0:T(8,128)(2,1)}, u32[]{:S(2)}, u32[]{:S(2)}) collective-permute-start(bf16[288,1024]{1,0:T(8,128)(2,1)} %get-tuple-element.88), channel_id=1, source_target_pairs={{0,24},{4,28},{8,16},{12,20},{16,8},{20,12},{24,0},{28,4},{1,25},{... | collective-permute-start | bytes 1769480 | tf_op jit(solution)/shard_map/ppermute | solution.py:465
  356.1 31.2 %collective-permute-start.14 = (bf16[288,1024]{1,0:T(8,128)(2,1)}, bf16[288,1024]{1,0:T(8,128)(2,1)}, u32[]{:S(2)}, u32[]{:S(2)}) collective-permute-start(bf16[288,1024]{1,0:T(8,128)(2,1)} %get-tuple-element.86), channel_id=1, source_target_pairs={{0,16},{4,20},{8,24},{12,28},{16,0},{20,4},{24,8},{28,12},{1,17},{... | collective-permute-start | bytes 1769480 | tf_op jit(solution)/shard_map/ppermute | solution.py:465
  357.1 33.2 %collective-permute-start.13 = (bf16[288,1024]{1,0:T(8,128)(2,1)}, bf16[288,1024]{1,0:T(8,128)(2,1)}, u32[]{:S(2)}, u32[]{:S(2)}) collective-permute-start(bf16[288,1024]{1,0:T(8,128)(2,1)} %get-tuple-element.84), channel_id=1, source_target_pairs={{0,8},{4,12},{8,0},{12,4},{16,24},{20,28},{24,16},{28,20},{1,9},{5... | collective-permute-start | bytes 1769480 | tf_op jit(solution)/shard_map/ppermute | solution.py:465
  361.9 48.3 %collective-permute-start.25 = (bf16[1,32,1024]{2,1,0:T(8,128)(2,1)S(1)}, bf16[1,32,1024]{2,1,0:T(8,128)(2,1)S(1)}, u32[]{:S(2)}, u32[]{:S(2)}) collective-permute-start(bf16[1,32,1024]{2,1,0:T(8,128)(2,1)S(1)} %bitcast.100), channel_id=1, source_target_pairs={{0,8},{4,12},{8,0},{12,4},{16,24},{20,28},{24,16},{28,20},{1,9},{5... | collective-permute-start | bytes 196616 | tf_op jit(solution)/shard_map/ppermute | solution.py:465
  367.7 44.4 %collective-permute-start.23 = (bf16[2,128,768]{2,1,0:T(8,128)(2,1)}, bf16[2,128,768]{2,1,0:T(8,128)(2,1)}, u32[]{:S(2)}, u32[]{:S(2)}) collective-permute-start(bf16[2,128,768]{2,1,0:T(8,128)(2,1)} %pad_maximum_fusion.5), channel_id=1, source_target_pairs={{0,16},{4,20},{8,24},{12,28},{16,0},{20,4},{24,8},{28,12},{1,17},{... | collective-permute-start | bytes 1179656 | tf_op jit(solution)/shard_map/ppermute | solution.py:465
  380.9 50.4 %collective-permute-start.35 = (bf16[4,3,176,512]{3,2,1,0:T(8,128)(2,1)S(1)}, bf16[4,3,176,512]{3,2,1,0:T(8,128)(2,1)}, u32[]{:S(2)}, u32[]{:S(2)}) collective-permute-start(bf16[4,3,176,512]{3,2,1,0:T(8,128)(2,1)S(1)} %pad_maximum_fusion.own_ref), channel_id=1, source_target_pairs={{0,4},{4,0},{8,12},{12,8},{16,20},{20,16},{24,28},{28,24},{1,5},{5... | collective-permute-start | bytes 6488072 | tf_op jit(solution)/shard_map/ppermute | solution.py:465
  400.2 1.2 collective-permute-start.16
  401.4 4.2 collective-permute-start.17
  405.5 3.7 collective-permute-start.18
  409.2 6.9 %collective-permute-start.21 = (f32[2051]{0:T(1024)S(1)}, f32[2051]{0:T(1024)S(1)}, u32[]{:S(2)}, u32[]{:S(2)}) collective-permute-start(f32[2051]{0:T(1024)S(1)} %bitcast.111), channel_id=1, source_target_pairs={{0,3},{1,0},{2,1},{3,2},{4,7},{5,4},{6,5},{7,6},{8,11},{9,8},{10,9... | collective-permute-start | bytes 24620 | tf_op jit(solution)/shard_map/ppermute | solution.py:470
  409.2 6.9 %collective-permute-start.20 = (f32[2051]{0:T(1024)S(1)}, f32[2051]{0:T(1024)S(1)}, u32[]{:S(2)}, u32[]{:S(2)}) collective-permute-start(f32[2051]{0:T(1024)S(1)} %bitcast.112), channel_id=1, source_target_pairs={{0,2},{1,3},{2,0},{3,1},{4,6},{5,7},{6,4},{7,5},{8,10},{9,11},{10,... | collective-permute-start | bytes 24620 | tf_op jit(solution)/shard_map/ppermute | solution.py:470
  410.3 5.9 %collective-permute-start.19 = (f32[2051]{0:T(1024)S(1)}, f32[2051]{0:T(1024)S(1)}, u32[]{:S(2)}, u32[]{:S(2)}) collective-permute-start(f32[2051]{0:T(1024)S(1)} %bitcast.113), channel_id=1, source_target_pairs={{0,1},{1,2},{2,3},{3,0},{4,5},{5,6},{6,7},{7,4},{8,9},{9,10},{10,1... | collective-permute-start | bytes 24620 | tf_op jit(solution)/shard_map/ppermute | solution.py:470
  412.1 5.0 %collective-permute-start.26 = (bf16[2,32,1024]{2,1,0:T(8,128)(2,1)S(1)}, bf16[2,32,1024]{2,1,0:T(8,128)(2,1)S(1)}, u32[]{:S(2)}, u32[]{:S(2)}) collective-permute-start(bf16[2,32,1024]{2,1,0:T(8,128)(2,1)S(1)} %pad_maximum_fusion.7), channel_id=1, source_target_pairs={{0,16},{4,20},{8,24},{12,28},{16,0},{20,4},{24,8},{28,12},{1,17},{... | collective-permute-start | bytes 393224 | tf_op jit(solution)/shard_map/ppermute | solution.py:465
  416.1 5.6 %collective-permute-start.24 = (bf16[4,128,768]{2,1,0:T(8,128)(2,1)}, bf16[4,128,768]{2,1,0:T(8,128)(2,1)}, u32[]{:S(2)}, u32[]{:S(2)}) collective-permute-start(bf16[4,128,768]{2,1,0:T(8,128)(2,1)} %pad_maximum_fusion.2), channel_id=1, source_target_pairs={{0,4},{4,0},{8,12},{12,8},{16,20},{20,16},{24,28},{28,24},{1,5},{5... | collective-permute-start | bytes 2359304 | tf_op jit(solution)/shard_map/ppermute | solution.py:465
  417.2 1.6 collective-permute-start.27
  (49 other events, 313.7 us)
Sparse Core Ops, SparseCore 0:
  62.0 63.8 all-gather.2
  255.5 68.5 reduce-scatter.1

commit v2 on v1

--- a/solution.py
+++ b/solution.py
@@ -15,6 +15,7 @@
 TN = (((0,), (0,)), ((), ()))
 F32 = jnp.float32
 BF16 = jnp.bfloat16
+SMALL = pl.CostEstimate(flops=1000, bytes_accessed=1000, transcendentals=0)
 
 
 def bucket_of(offset):
@@ -161,7 +162,7 @@
             pltpu.VMEM((length, TILE), F32),
         ],
         compiler_params=pltpu.CompilerParams(vmem_limit_bytes=40 << 20),
-        cost_estimate=pl.CostEstimate(flops=20_000_000_000, bytes_accessed=4_000_000, transcendentals=5_000_000),
+        cost_estimate=SMALL,
         name="attn_fwd",
     )(seg, bias, qkv, tiles)
 
@@ -273,7 +274,7 @@
             pltpu.VMEM((length, width), F32),
         ],
         compiler_params=pltpu.CompilerParams(vmem_limit_bytes=48 << 20),
-        cost_estimate=pl.CostEstimate(flops=40_000_000_000, bytes_accessed=6_000_000, transcendentals=5_000_000),
+        cost_estimate=SMALL,
         name="attn_bwd",
     )(seg, bias, qkv, o, do, lse, tiles)
 
@@ -348,9 +349,7 @@
         out_specs=(vmem,) * 5,
         scratch_shapes=[pltpu.VMEM((units, width), BF16)] * 3 + [pltpu.SemaphoreType.DMA((3, 2 * ring))],
         compiler_params=pltpu.CompilerParams(vmem_limit_bytes=40 << 20),
-        cost_estimate=pl.CostEstimate(
-            flops=16 * tokens * width * units, bytes_accessed=6 * units * width + 10 * tokens * width, transcendentals=tokens * units
-        ),
+        cost_estimate=SMALL,
         name="ffn",
     )(where, x, c, mine, other)
 
@@ -404,60 +403,167 @@
         out_specs=(vmem, vmem),
         scratch_shapes=[inner, wide, inner, wide, inner, pltpu.SemaphoreType.DMA((5, n))],
         compiler_params=pltpu.CompilerParams(vmem_limit_bytes=48 << 20),
-        cost_estimate=pl.CostEstimate(
-            flops=6 * n * rows * width * units, bytes_accessed=4 * n * rows * width + 6 * n * rows * units, transcendentals=0
-        ),
+        cost_estimate=SMALL,
         name="ffn_grads",
     )(where, *hs, *cs, *gs, *xs, *us)
 
 
-def place_kernel(masks, where_ref, own_ref, other_ref, gate_ref, up_ref, down_ref):
+def out_grads_kernel(where_ref, o_ref, d_ref, keep_ref, give_ref, held):
     core, chip = where_ref[0], where_ref[1]
-    _, _, units, half = own_ref.shape
-    for m, out_ref in enumerate((gate_ref, up_ref, down_ref)):
-        for r, mask in enumerate(masks):
-            rows = pl.ds(pl.multiple_of((chip ^ mask) * units, 8), units)
+    chips, ring, rows, half = keep_ref.shape
+    for n, out_ref in enumerate((give_ref, keep_ref)):
+        start = pl.multiple_of((core ^ (1 - n)) * half, 128)
+        held[...] = lax.dot_general(
+            o_ref[...], d_ref[:, pl.ds(start, half)], TN, preferred_element_type=F32
+        ).astype(BF16)
+        for r in range(chips):
+            for q in range(ring):
+                first = (q * chips + (chip ^ r)) * rows
+                out_ref[r, q] = held[pl.ds(pl.multiple_of(first, rows), rows)]
+
+
+def out_grads(where, o, d, ring):
+    width = d.shape[1]
+    vmem = pl.BlockSpec(memory_space=pltpu.VMEM)
+    shape = jax.ShapeDtypeStruct((4, ring, o.shape[1] // (4 * ring), width // 2), BF16)
+    return pl.pallas_call(
+        out_grads_kernel,
+        out_shape=(shape, shape),
+        in_specs=[pl.BlockSpec(memory_space=pltpu.SMEM), vmem, vmem],
+        out_specs=(vmem, vmem),
+        scratch_shapes=[pltpu.VMEM((o.shape[1], width // 2), BF16)],
+        compiler_params=pltpu.CompilerParams(vmem_limit_bytes=24 << 20),
+        cost_estimate=SMALL,
+        name="out_grads",
+    )(where, o, d)
+
+
+def normed_grad_kernel(d_ref, w_ref, out_ref):
+    out_ref[...] = lax.dot_general(d_ref[...], w_ref[...], NT, preferred_element_type=F32).astype(BF16)
+
+
+def normed_grad(d, w):
+    vmem = pl.BlockSpec(memory_space=pltpu.VMEM)
+    return pl.pallas_call(
+        normed_grad_kernel,
+        out_shape=jax.ShapeDtypeStruct((d.shape[0], w.shape[0]), BF16),
+        in_specs=[vmem, vmem],
+        out_specs=vmem,
+        compiler_params=pltpu.CompilerParams(vmem_limit_bytes=24 << 20),
+        cost_estimate=SMALL,
+        name="normed_grad",
+    )(d, w)
+
+
+def qkv_grads_kernel(where_ref, x_ref, d_ref, w_ref, keep_ref, give_ref, gain_ref):
+    core, chip = where_ref[0], where_ref[1]
+    chips, rows, _ = keep_ref.shape
+    for n, out_ref in enumerate((give_ref, keep_ref)):
+        for r in range(chips):
+            block = (core ^ (1 - n)) * chips + (chip ^ r)
+            start = pl.multiple_of(block * rows, 128)
+            grad = lax.dot_general(x_ref[:, pl.ds(start, rows)], d_ref[...], TN, preferred_element_type=F32)
+            out_ref[r] = grad.astype(BF16)
+            line = jnp.sum(grad * w_ref[pl.ds(start, rows)].astype(F32), axis=1, keepdims=True)
+            gain_ref[pl.ds(block, 1)] = jnp.transpose(jnp.broadcast_to(line, (rows, rows)))[:1]
+
+
+def qkv_grads(where, x, d, w):
+    rows = x.shape[1] // 8
+    vmem = pl.BlockSpec(memory_space=pltpu.VMEM)
+    shape = jax.ShapeDtypeStruct((4, rows, d.shape[1]), BF16)
+    return pl.pallas_call(
+        qkv_grads_kernel,
+        out_shape=(shape, shape, jax.ShapeDtypeStruct((8, rows), F32)),
+        in_specs=[pl.BlockSpec(memory_space=pltpu.SMEM), vmem, vmem, vmem],
+        out_specs=(vmem,) * 3,
+        compiler_params=pltpu.CompilerParams(vmem_limit_bytes=24 << 20),
+        cost_estimate=SMALL,
+        name="qkv_grads",
+    )(where, x, d, w)
+
+
+def place_kernel(where_ref, own_ref, other_ref, *out_refs):
+    core, chip = where_ref[0], where_ref[1]
+    chips, _, half = own_ref.shape
+    first = 0
+    for target in out_refs:
+        units = target.shape[0] // chips
+        for r in range(chips):
+            rows = pl.ds(pl.multiple_of((chip ^ r) * units, 8), units)
             for n, ref in enumerate((own_ref, other_ref)):
                 columns = pl.ds(pl.multiple_of((core ^ n) * half, 128), half)
-                out_ref[rows, columns] = ref[r, m].astype(F32)
-
-
-def place(where, own, other, masks):
-    _, _, units, half = own.shape
-    vmem = pl.BlockSpec(memory_space=pltpu.VMEM)
-    shape = jax.ShapeDtypeStruct((4 * units, 2 * half), F32)
-    return pl.pallas_call(
-        functools.partial(place_kernel, masks),
-        out_shape=(shape,) * 3,
+                target[rows, columns] = ref[r, first : first + units].astype(F32)
+        first += units
+
+
+def place(where, own, other, sizes):
+    chips, _, half = own.shape
+    vmem = pl.BlockSpec(memory_space=pltpu.VMEM)
+    return pl.pallas_call(
+        place_kernel,
+        out_shape=tuple(jax.ShapeDtypeStruct((chips * size, 2 * half), F32) for size in sizes),
         in_specs=[pl.BlockSpec(memory_space=pltpu.SMEM), vmem, vmem],
-        out_specs=(vmem,) * 3,
+        out_specs=(vmem,) * len(sizes),
         compiler_params=pltpu.CompilerParams(vmem_limit_bytes=40 << 20),
-        cost_estimate=pl.CostEstimate(flops=0, bytes_accessed=12 * own.size * 2, transcendentals=0),
+        cost_estimate=SMALL,
         name="place",
     )(where, own, other)
 
 
-def place_rows_kernel(masks, where_ref, pieces_ref, *out_refs):
-    _, rows, width = pieces_ref.shape
-    part = width // len(out_refs)
-    for r, mask in enumerate(masks):
-        target = pl.ds(pl.multiple_of((where_ref[2] ^ mask) * rows, 8), rows)
-        value = pieces_ref[r].astype(F32)
-        for i, out_ref in enumerate(out_refs):
-            out_ref[target] = value[:, i * part : (i + 1) * part]
-
-
-def place_rows(where, pieces, masks, n_out):
-    count, rows, width = pieces.shape
-    vmem = pl.BlockSpec(memory_space=pltpu.VMEM)
-    return pl.pallas_call(
-        functools.partial(place_rows_kernel, masks),
-        out_shape=(jax.ShapeDtypeStruct((count * rows, width // n_out), F32),) * n_out,
-        in_specs=[pl.BlockSpec(memory_space=pltpu.SMEM), vmem],
-        out_specs=(vmem,) * n_out,
-        cost_estimate=pl.CostEstimate(flops=0, bytes_accessed=6 * pieces.size, transcendentals=0),
-        name="place_rows",
-    )(where, pieces)
+def place_late_kernel(where_ref, own_ref, other_ref, *out_refs):
+    core, chip = where_ref[0], where_ref[1]
+    chips, total, width = own_ref.shape
+    projections, out_ref = out_refs[:3], out_refs[3]
+    rows = projections[0].shape[0] // (2 * chips)
+    part, half = width // 3, out_ref.shape[1] // 2
+    for n, ref in enumerate((own_ref, other_ref)):
+        for r in range(chips):
+            start = ((core ^ n) * chips + (chip ^ r)) * rows
+            value = ref[r, :rows].astype(F32)
+            for i, target in enumerate(projections):
+                target[pl.ds(pl.multiple_of(start, 8), rows)] = value[:, i * part : (i + 1) * part]
+            start = pl.multiple_of((chip ^ r) * (total - rows), 8)
+            columns = pl.ds(pl.multiple_of((core ^ n) * half, 128), half)
+            out_ref[pl.ds(start, total - rows), columns] = ref[r, rows:, :half].astype(F32)
+
+
+def place_late(where, own, other, rows, half):
+    chips, total, width = own.shape
+    vmem = pl.BlockSpec(memory_space=pltpu.VMEM)
+    projection = jax.ShapeDtypeStruct((2 * chips * rows, width // 3), F32)
+    return pl.pallas_call(
+        place_late_kernel,
+        out_shape=(projection,) * 3 + (jax.ShapeDtypeStruct((chips * (total - rows), 2 * half), F32),),
+        in_specs=[pl.BlockSpec(memory_space=pltpu.SMEM), vmem, vmem],
+        out_specs=(vmem,) * 4,
+        cost_estimate=SMALL,
+        name="place_late",
+    )(where, own, other)
+
+
+def place_out_kernel(where_ref, mine_ref, other_ref, out_ref):
+    chips, ring, rows, _ = mine_ref.shape
+    core, chip, z = where_ref[0], where_ref[1], where_ref[3]
+    for s in range(ring):
+        quarter = lax.rem(z + ring - s, ring)
+        for r in range(chips):
+            for n, ref in enumerate((mine_ref, other_ref)):
+                start = ((quarter * chips + (chip ^ r)) * 2 + (core ^ n)) * rows
+                out_ref[pl.ds(pl.multiple_of(start, rows), rows)] = ref[r, s]
+
+
+def place_out(where, mine, other):
+    chips, ring, rows, width = mine.shape
+    vmem = pl.BlockSpec(memory_space=pltpu.VMEM)
+    return pl.pallas_call(
+        place_out_kernel,
+        out_shape=jax.ShapeDtypeStruct((2 * chips * ring * rows, width), mine.dtype),
+        in_specs=[pl.BlockSpec(memory_space=pltpu.SMEM), vmem, vmem],
+        out_specs=vmem,
+        cost_estimate=SMALL,
+        name="place_out",
+    )(where, mine, other)
 
 
 def swap(value, mask):
@@ -483,14 +589,6 @@
     while bit < lax.axis_size("dp"):
         yield bit
         bit *= 2
-
-
-def gather_all(piece):
-    pieces, masks = piece[None], [0]
-    for bit in (*bits_from(2), 1):
-        pieces = jnp.concatenate([pieces, swap(pieces, bit)], axis=0)
-        masks = masks + [mask | bit for mask in masks]
-    return pieces, tuple(masks)
 
 
 def sum_rows(value):
@@ -544,24 +642,22 @@
     dp = lax.axis_index("dp")
     core = dp & 1
     chip = (dp >> 1) & 3
-    where = jnp.stack([core, chip, dp]).astype(jnp.int32)
+    where = jnp.stack([core, chip, dp, z]).astype(jnp.int32)
 
     x_low = tokens.reshape(shard, width)
     cot = cotangent.reshape(shard, width)
     row_tiles, col_tiles = bias_tiles(rel_bias)
     w_qkv = jnp.concatenate([w_query, w_key, w_value], axis=1)
 
-    blocks = [x_low]
+    out_rows = feats // 8
+    out_piece = lax.dynamic_slice_in_dim(w_out, (2 * chip + core) * out_rows, out_rows, 0)
+    blocks = [jnp.concatenate([x_low, out_piece], axis=0)]
+    blocks.append(shift(blocks[-1], 1))
+    cs = to_chips(after(cot, blocks[1]))
     blocks.append(shift(blocks[-1], 1))
     blocks.append(shift(blocks[-1], 1))
-    cs = to_chips(cot)
-    blocks.append(shift(after(blocks[-1], *cs), 1))
-    out_rows = feats // n_dp
-    out_piece = lax.dynamic_slice_in_dim(w_out, dp * out_rows, out_rows, 0)
-    out_ring = lax.all_to_all(jnp.broadcast_to(out_piece, (ring, *out_piece.shape)), "tensor", 0, 0, tiled=True)
-    out_ring = after(out_ring, *cs)
-    out_all = lax.all_to_all(jnp.broadcast_to(out_ring, (n_dp, *out_ring.shape)), "dp", 0, 0, tiled=True)
-    out_all = jnp.moveaxis(out_all, 0, 1).reshape(ring * feats, width)
+    out_ring = jnp.stack([block[shard:] for block in blocks])
+    out_chips = to_chips(out_ring)
 
     def unit_rows(array):
         return lax.dynamic_slice(array, (chip * (units // 4), core * (width // 2)), (units // 4, width // 2))
@@ -574,39 +670,53 @@
         ],
         axis=0,
     )
-    mine_w = lax.all_gather(after(pack, blocks[2]), "tensor", axis=0)
-    other_w = swap(mine_w, 1)
+    mine_w = lax.all_gather(after(pack, blocks[3]), "tensor", axis=0)
 
     qkv = jnp.zeros((length, 3 * feats), BF16)
     norm_full = jnp.zeros((length, width), BF16)
     for s, block in enumerate(blocks):
-        values = block.astype(F32)
+        values = block[:shard].astype(F32)
         normed = (values * inverse_rms(values) * norm1_gain).astype(BF16)
         start = ((z - s) % ring) * shard
         norm_full = lax.dynamic_update_slice_in_dim(norm_full, normed, start, 0)
         qkv = lax.dynamic_update_slice_in_dim(qkv, dot(normed, w_qkv).astype(BF16), start, 0)
 
-    o_row, lse = attn_fwd(segment_ids, rel_bias, qkv, row_tiles)
+    o_row, lse = attn_fwd(segment_ids, rel_bias, after(qkv, *cs), row_tiles)
+    out_mine = after(jnp.stack(out_chips), o_row)
+    out_all = place_out(where, out_mine, swap(out_mine, 1))
     o_home = lax.all_to_all(o_row, "tensor", 0, 1, tiled=True)
     attn = dot(o_home, out_all)
     x_one = x_low.astype(F32) + attn
     r_two = inverse_rms(x_one)
     norm_two = (x_one * r_two * norm2_gain).astype(BF16)
 
+    mine_w = after(mine_w, norm_two)
+    other_w = swap(mine_w, 1)
     xs = to_chips(norm_two)
-    parts = [ffn(where, x, c, mine_w, other_w) for x, c in zip(xs, cs)]
-
+    parts = []
+    for x, c in zip(xs, cs):
+        if parts:
+            x = after(x, parts[-1][0])
+        parts.append(ffn(where, x, c, mine_w, other_w))
+
+    def returns(which, *others):
+        terms = [after(part[which], *others) if others else part[which] for part in parts]
+        return [terms[0]] + [swap(terms[mask], 2 * mask) for mask in CHIPS[1:]]
+
+    def total_of(terms):
+        return sum(term.astype(F32) for term in terms)
+
+    back = returns(0)
     keep, give = ffn_grads(
-        where, [part[2] for part in parts], cs, [part[3] for part in parts], xs, [part[4] for part in parts], ring
+        where,
+        [part[2] for part in parts],
+        cs,
+        [part[3] for part in parts],
+        xs,
+        [part[4] for part in parts],
+        ring,
     )
-
-    def sum_chips(terms):
-        total = terms[0].astype(F32)
-        for mask in CHIPS[1:]:
-            total = total + swap(terms[mask], 2 * mask).astype(F32)
-        return total
-
-    d_two = sum_chips([after(parts[0][0], keep)] + [part[0] for part in parts[1:]])
+    d_two = total_of([after(back[0], keep)] + back[1:])
     u_two = d_two * norm2_gain
     d_x_one = cot.astype(F32) + r_two * u_two - x_one * (
         r_two * r_two * r_two * jnp.mean(u_two * x_one, axis=-1, keepdims=True)
@@ -614,15 +724,61 @@
     d_attn = d_x_one.astype(BF16)
     d_o = dot(d_attn, out_all, NT).astype(BF16)
     do_row = lax.all_to_all(d_o, "tensor", 1, 0, tiled=True)
-    ffo = sum_chips([after(part[1], d_o) for part in parts])
+
+    give, o_done = after(give, d_o), after(o_home, d_o)
+    keep = add(keep, swap(give, 1))
+    ffn_piece = lax.psum_scatter(keep, "tensor", scatter_dimension=0).reshape(-1, width // 2)
+
+    def sum_chips(pieces):
+        return total_of([pieces[0]] + [swap(pieces[r], 2 * r) for r in CHIPS[1:]])
+
+    out_keep, out_give = out_grads(where, o_done, d_attn, ring)
+    out_keep = add(out_keep, swap(out_give, 1))
+    got = sum_chips(out_keep).astype(BF16)
+    ffo_back = returns(1, out_keep)
+    ffo = total_of(ffo_back)
     y = x_one + ffo
     out_tokens = y.astype(BF16)
     grad_two = jnp.sum(d_two * x_one * r_two, axis=0)
     stats = jnp.stack([jnp.sum(attn * attn), jnp.sum(ffo * ffo), jnp.sum(y * y)])
 
     dqkv, near, far = attn_bwd(segment_ids, rel_bias, qkv, o_row, do_row, lse, col_tiles)
-    d_one_part = dot(dqkv, w_qkv, NT).astype(BF16)
+    dqkv = after(dqkv, ffn_piece, got, *ffo_back)
+    d_one_part = normed_grad(dqkv, w_qkv)
     d_one = lax.psum_scatter(d_one_part, "tensor", scatter_dimension=0, tiled=True).astype(F32)
+    piece = after(ffn_piece, dqkv)
+    for bit in bits_from(8):
+        piece = add(piece, swap(piece, bit))
+    own = jnp.stack(to_chips(piece))
+
+    qkv_keep, qkv_give, grad_one = qkv_grads(where, norm_full, after(dqkv, d_one_part), w_qkv)
+    qkv_piece = sum_chips(add(qkv_keep, swap(qkv_give, 1))).astype(BF16)
+    got = after(got, dqkv)
+    out_parts = [lax.dynamic_index_in_dim(got, (z + s) % ring, 0, keepdims=False) for s in range(ring)]
+    out_piece = total_of([out_parts[0]] + [shift(out_parts[s], s) for s in range(1, ring)]).astype(BF16)
+    late = jnp.concatenate(
+        [qkv_piece, jnp.pad(out_piece, ((0, 0), (0, 3 * feats - width // 2)))], axis=0
+    )
+    for bit in bits_from(8):
+        late = add(late, swap(late, bit))
+    grad_gate, grad_up, grad_down = place(where, own, swap(own, 1), (units // 4,) * 3)
+    grad_gate, grad_up = jnp.transpose(grad_gate), jnp.transpose(grad_up)
+    late = jnp.stack(to_chips(after(late, own)))
+    grad_query, grad_key, grad_value, grad_out = place_late(where, late, swap(late, 1), width // 8, width // 2)
+
+    near = after(near, qkv_give)
+    row = width // 8
+    stats = jnp.pad(stats, (0, row - 3)).reshape(1, row)
+    small = jnp.concatenate([grad_two.reshape(8, row), grad_one, stats, bias_grad(near, far)], axis=0)
+    small = sum_rows(small)
+    grad_bias = small[17:, :heads]
+    small = sum_ring(small[:17])
+    grad_norm2, grad_norm1 = small[:8].reshape(width), small[8:16].reshape(width) / norm1_gain
+    stat_sums = small[16, :3]
+    count = shard * rows_here * width * n_dp * ring
+    rms_stats = jnp.sqrt(stat_sums / count)
+
+    d_one = after(d_one, grad_query, small, grad_bias)
     x_in = x_low.astype(F32)
     r_one = inverse_rms(x_in)
     u_one = d_one * norm1_gain
@@ -630,40 +786,6 @@
         d_x_one + r_one * u_one - x_in * (r_one * r_one * r_one * jnp.mean(u_one * x_in, axis=-1, keepdims=True))
     ).astype(BF16)
 
-    keep = add(keep, swap(give, 1))
-
-    def share_of(s):
-        return lax.dynamic_index_in_dim(keep, (z - s) % ring, 0, keepdims=False)
-
-    piece = after(share_of(1), d_o)
-    for s in (2, 3, 0):
-        piece = add(shift(piece, 1), share_of(s))
-    for bit in bits_from(8):
-        piece = add(piece, swap(piece, bit))
-    own = jnp.stack(to_chips(piece))
-    grad_gate, grad_up, grad_down = place(where, own, swap(own, 1), CHIPS)
-    grad_gate, grad_up = jnp.transpose(grad_gate), jnp.transpose(grad_up)
-
-    grad_o = dot(o_home, d_attn, TN).astype(BF16).reshape(ring, n_dp, out_rows, width)
-    got = lax.all_to_all(jnp.moveaxis(grad_o, 1, 0), "dp", 0, 0, tiled=True)
-    got = jnp.sum(got.astype(F32), axis=0).astype(BF16)
-    got = lax.all_to_all(got, "tensor", 0, 0, tiled=True)
-    pieces, masks = gather_all(jnp.sum(got.astype(F32), axis=0).astype(BF16))
-    (grad_out,) = place_rows(where, pieces, masks, 1)
-
-    grad_qkv = dot(norm_full, after(dqkv, d_one_part), TN)
-    grad_one = jnp.sum(grad_qkv * w_qkv.astype(F32), axis=1) / norm1_gain
-    got = lax.all_to_all(grad_qkv.astype(BF16).reshape(n_dp, width // n_dp, 3 * feats), "dp", 0, 0, tiled=True)
-    pieces, masks = gather_all(jnp.sum(got.astype(F32), axis=0).astype(BF16))
-    grad_query, grad_key, grad_value = place_rows(where, pieces, masks, 3)
-
-    small = jnp.concatenate([grad_two, stats, grad_one, bias_grad(near, far)[:, :heads].reshape(-1)])
-    small = sum_rows(small)
-    grad_bias = small[2 * width + 3 :].reshape(-1, heads)
-    small = sum_ring(small[: 2 * width + 3])
-    grad_norm2, stat_sums, grad_norm1 = small[:width], small[width : width + 3], small[width + 3 :]
-    count = shard * rows_here * width * n_dp * ring
-    rms_stats = jnp.sqrt(stat_sums / count)
     shape = (shard, rows_here, width)
     return (
         out_tokens.reshape(shape),

time: 452 us -> 391 us (0.87)
  waiting for transfers between devices: 193 us -> 156 us
  starting transfers between devices: 76 us -> 61.9 us
  matrix products: 21.5 us -> 8.79 us
  Pallas kernels: 74.1 us -> 85.8 us
  other arithmetic: 38.3 us -> 29.9 us
    ppermute x9, waiting for transfers between devices: 92 us -> 49.6 us  [shift(): lax.ppermute(value, 'tensor', [(i, (i + step) % size) for i in range(size)])]
    all_to_all x1, waiting for transfers between devices: 0.01 us -> 29.7 us  [local(): o_home = lax.all_to_all(o_row, 'tensor', 0, 1, tiled=True)]
    all_gather x1, waiting for transfers between devices: 29 us -> 0.02 us  [local(): mine_w = lax.all_gather(after(pack, blocks[3]), 'tensor', axis=0)]
    all_to_all x5 -> x0, starting transfers between devices: 28.2 us -> none  [the longest x1 11.5 us: local(): lax.all_to_all(grad_qkv.astype(BF16).reshape(n_dp, width // n_dp, 3 * fea...]
    ppermute x27 -> x37, starting transfers between devices: 29.2 us -> 47.3 us  [swap(): return lax.ppermute(value, 'dp', [(i, i ^ mask) for i in range(size)])]
    dot_general x9 -> x6, matrix products: 21.5 us -> 8.79 us  [dot(): return lax.dot_general(left, right, dims, preferred_element_type=F32)]
    pallas_call x3 -> x6, Pallas kernels: 11 us -> 22.4 us  [the longest x1 5.59 us: place(): pl.pallas_call(place_kernel, out_shape=tuple((jax.ShapeDtypeStruct((chips...]
    all_to_all x1, waiting for transfers between devices: 8.45 us -> 19.2 us  [local(): do_row = lax.all_to_all(d_o, 'tensor', 1, 0, tiled=True)]
  transfers between devices with their start and end apart: 45 -> 51, of which waited for: 22 -> 24; matrix products, arithmetic and copies ran while one was open for 17% -> 10% of each run, Pallas kernels for 15% -> 20%
where the time goes in v2:
time: 391 us; the launch traced here: 385 us
  waiting for transfers between devices  156 us (40%)
  Pallas kernels  85.8 us (22%)
  starting transfers between devices  61.9 us (16%)
  other arithmetic  29.9 us (8%)
  local copies, waits for them, and re-layouts  27.5 us (7%)
  between operations  15.2 us (4%)
  matrix products  8.79 us (2%)
    ppermute x37, waiting for transfers between devices, swap(): return lax.ppermute(value, 'dp', [(i, i ^ mask) for i in range(size)])  57.6 us
    ppermute x9, waiting for transfers between devices, shift(): lax.ppermute(value, 'tensor', [(i, (i + step) % size) for i in range(size)])  49.6 us
    ppermute x37, starting transfers between devices, swap(): return lax.ppermute(value, 'dp', [(i, i ^ mask) for i in range(size)])  47.3 us
    all_to_all x1, waiting for transfers between devices, local(): o_home = lax.all_to_all(o_row, 'tensor', 0, 1, tiled=True)  29.7 us
    pallas_call x4, Pallas kernels, ffn(): pl.pallas_call(ffn_kernel, out_shape=(wide, wide, inner, inner, inner), i...  26.2 us
    all_to_all x1, waiting for transfers between devices, local(): do_row = lax.all_to_all(d_o, 'tensor', 1, 0, tiled=True)  19.2 us
    unnamed x130, local copies, waits for them, and re-layouts  19.1 us
    pallas_call x1, Pallas kernels, ffn_grads(): pl.pallas_call(functools.partial(ffn_grads_kernel, n), out_shape=(shape,...  11.6 us
  transfers between devices with their start and end apart: 51, of which 24 were waited for; matrix products, arithmetic and copies ran while one was open for 10% of the time, Pallas kernels for 20%

profile of v2, /device:TPU:0, one launch (start us, length us, event | category | flops | bytes accessed | tf_op | source)
XLA Modules:
  0.0 385.2 jit_solution(1857811164266310804)
XLA Ops:
  10.2 3.0 collective-permute-start
  14.0 5.2 %bias_tiles.1 = (f32[4,3,128,128]{3,2,1,0:T(8,128)}, f32[4,3,128,128]{3,2,1,0:T(8,128)}) custom-call(f32[32,4]{1,0:T(8,128)} %copy.33.bias_ref), custom_call_target="tpu_custom_call" | custom-call | tf_op jit(solution)/shard_map/bias_tiles/pallas_call | solution.py:49
  25.4 4.9 %collective-permute-done = bf16[320,1024]{1,0:T(8,128)(2,1)} collective-permute-done((bf16[320,1024]{1,0:T(8,128)(2,1)}, bf16[320,1024]{1,0:T(8,128)(2,1)}, u32[]{:S(2)}, u32[]{:S(2)}) %collective-permute-start) | collective-permute-done | bytes 655392 | tf_op jit(solution)/shard_map/ppermute | solution.py:576
  37.8 14.5 %collective-permute-done.1 = bf16[320,1024]{1,0:T(8,128)(2,1)S(1)} collective-permute-done((bf16[320,1024]{1,0:T(8,128)(2,1)}, bf16[320,1024]{1,0:T(8,128)(2,1)S(1)}, u32[]{:S(2)}, u32[]{:S(2)}) %collective-permute-start.1) | collective-permute-done | bytes 655392 | tf_op jit(solution)/shard_map/ppermute | solution.py:576
  53.4 15.1 %collective-permute-done.2 = bf16[320,1024]{1,0:T(8,128)(2,1)} collective-permute-done((bf16[320,1024]{1,0:T(8,128)(2,1)S(1)}, bf16[320,1024]{1,0:T(8,128)(2,1)}, u32[]{:S(2)}, u32[]{:S(2)}) %collective-permute-start.2) | collective-permute-done | bytes 655392 | tf_op jit(solution)/shard_map/ppermute | solution.py:576
  70.4 2.0 collective-permute-start.8
  77.2 7.7 %attn_fwd.1 = (bf16[1152,256]{1,0:T(8,128)(2,1)S(1)}, f32[4,8,1152]{2,1,0:T(8,128)S(1)}) custom-call(s32[1,1152]{1,0:T(1,128)S(1)} %copy-done.35, f32[32,4]{1,0:T(8,128)S(1)} %copy-done.29, bf16[1152,768]{1,0:T(8,128)(2,1)S(1)} %fusion.qkv_ref, f32[4,3,128,128]{3,2,1,0:T(8,128)S(1)} %copy-done.26), custom_call_target="tpu_custom_call" | custom-call | flops 1000 | bytes 1000 | tf_op jit(solution)/shard_map/attn_fwd/pallas_call | solution.py:151
  86.1 5.0 %collective-permute-start.9 = (bf16[4,4,32,1024]{3,2,1,0:T(8,128)(2,1)}, bf16[4,4,32,1024]{3,2,1,0:T(8,128)(2,1)}, u32[]{:S(2)}, u32[]{:S(2)}) collective-permute-start(bf16[4,4,32,1024]{3,2,1,0:T(8,128)(2,1)} %pad_maximum_fusion.2.mine_ref), channel_id=1, source_target_pairs={{0,4},{4,0},{8,12},{12,8},{16,20},{20,16},{24,28},{28,24},{1,5},{5... | collective-permute-start | bytes 3145736 | tf_op jit(solution)/shard_map/ppermute | solution.py:571
  91.1 3.5 all-to-all-start
  95.2 29.7 %all-to-all-done = bf16[4,288,256]{2,1,0:T(8,128)(2,1)S(1)} async-done(((bf16[4,288,256]{2,1,0:T(8,128)(2,1)}), bf16[4,288,256]{2,1,0:T(8,128)(2,1)S(1)}, u32[]{:S(2)}, u32[]{:S(2)}) %all-to-all-start) | async-done | bytes 589856 | tf_op jit(solution)/shard_map/all_to_all | solution.py:687
  125.0 3.1 place_out.1
  128.1 3.1 multiply_reduce_fusion.5
  132.5 2.5 collective-permute-start.11
  138.6 5.8 %ffn.4 = (bf16[288,1024]{1,0:T(8,128)(2,1)S(1)}, bf16[288,1024]{1,0:T(8,128)(2,1)S(1)}, bf16[288,704]{1,0:T(8,128)(2,1)S(1)}, bf16[288,704]{1,0:T(8,128)(2,1)S(1)}, bf16[288,704]{1,0:T(8,128)(2,1)S(1)}) custom-call(s32[4]{0:T(128)S(1)} %copy-done.32, bf16[288,1024]{1,0:T(8,128)(2,1)S(1)} %multiply_convert_fusion.x_ref.refs_12_, ...), custom_call_target="tpu_custom_call" | custom-call | flops 1000 | bytes 1000 | tf_op jit(solution)/shard_map/ffn/pallas_call | solution.py:345
  145.3 3.9 %collective-permute-done.11.x_ref.refs_13_ = bf16[288,1024]{1,0:T(8,128)(2,1)S(1)} collective-permute-done((bf16[288,1024]{1,0:T(8,128)(2,1)S(1)}, bf16[288,1024]{1,0:T(8,128)(2,1)S(1)}, u32[]{:S(2)}, u32[]{:S(2)}) %collective-permute-start.11) | collective-permute-done | bytes 589856 | tf_op jit(solution)/shard_map/ppermute | solution.py:571
  149.2 6.2 %ffn.5 = (bf16[288,1024]{1,0:T(8,128)(2,1)S(1)}, bf16[288,1024]{1,0:T(8,128)(2,1)}, bf16[288,704]{1,0:T(8,128)(2,1)S(1)}, bf16[288,704]{1,0:T(8,128)(2,1)S(1)}, bf16[288,704]{1,0:T(8,128)(2,1)S(1)}) custom-call(s32[4]{0:T(128)S(1)} %copy-done.32, bf16[288,1024]{1,0:T(8,128)(2,1)S(1)} %collective-permute-done.11.x_ref.refs_13_, ...), custom_call_target="tpu_custom_call" | custom-call | flops 1000 | bytes 1000 | tf_op jit(solution)/shard_map/ffn/pallas_call | solution.py:345
  155.4 7.6 %collective-permute-done.12.x_ref.refs_14_ = bf16[288,1024]{1,0:T(8,128)(2,1)S(1)} collective-permute-done((bf16[288,1024]{1,0:T(8,128)(2,1)S(1)}, bf16[288,1024]{1,0:T(8,128)(2,1)S(1)}, u32[]{:S(2)}, u32[]{:S(2)}) %collective-permute-start.12) | collective-permute-done | bytes 589856 | tf_op jit(solution)/shard_map/ppermute | solution.py:571
  163.0 7.0 %ffn.6 = (bf16[288,1024]{1,0:T(8,128)(2,1)S(1)}, bf16[288,1024]{1,0:T(8,128)(2,1)}, bf16[288,704]{1,0:T(8,128)(2,1)S(1)}, bf16[288,704]{1,0:T(8,128)(2,1)S(1)}, bf16[288,704]{1,0:T(8,128)(2,1)S(1)}) custom-call(s32[4]{0:T(128)S(1)} %copy-done.32, bf16[288,1024]{1,0:T(8,128)(2,1)S(1)} %collective-permute-done.12.x_ref.refs_14_, ...), custom_call_target="tpu_custom_call" | custom-call | flops 1000 | bytes 1000 | tf_op jit(solution)/shard_map/ffn/pallas_call | solution.py:345
  170.1 7.1 %ffn.7 = (bf16[288,1024]{1,0:T(8,128)(2,1)S(1)}, bf16[288,1024]{1,0:T(8,128)(2,1)}, bf16[288,704]{1,0:T(8,128)(2,1)S(1)}, bf16[288,704]{1,0:T(8,128)(2,1)S(1)}, bf16[288,704]{1,0:T(8,128)(2,1)S(1)}) custom-call(s32[4]{0:T(128)S(1)} %copy-done.32, bf16[288,1024]{1,0:T(8,128)(2,1)S(1)} %collective-permute-done.13.x_ref.refs_15_, ...), custom_call_target="tpu_custom_call" | custom-call | flops 1000 | bytes 1000 | tf_op jit(solution)/shard_map/ffn/pallas_call | solution.py:345
  180.8 11.6 %ffn_grads.1 = (bf16[4,3,176,512]{3,2,1,0:T(8,128)(2,1)}, bf16[4,3,176,512]{3,2,1,0:T(8,128)(2,1)}) custom-call(s32[4]{0:T(128)S(1)} %copy-done.32, bf16[288,704]{1,0:T(8,128)(2,1)S(1)} %get-tuple-element.85.refs_0_, bf16[288,704]{1,0:T(8,128)(2,1)S(1)} %get-tuple-element.87.refs_1_, bf16[288,704]{1,0:T(8,128)(2,1)S(1)} %get-tuple-element.90.refs_2_, ...), custom_call_target="tpu_custom_call" | custom-call | flops 1000 | bytes 1000 | tf_op jit(solution)/shard_map/ffn_grads/pallas_call | solution.py:399
  192.4 2.0 collective-permute-done.16
  194.4 9.7 %collective-permute-done.15 = bf16[288,1024]{1,0:T(8,128)(2,1)S(1)} collective-permute-done((bf16[288,1024]{1,0:T(8,128)(2,1)S(1)}, bf16[288,1024]{1,0:T(8,128)(2,1)S(1)}, u32[]{:S(2)}, u32[]{:S(2)}) %collective-permute-start.15) | collective-permute-done | bytes 589856 | tf_op jit(solution)/shard_map/ppermute | solution.py:571
  208.9 4.2 %collective-permute-done.21 = bf16[4,3,176,512]{3,2,1,0:T(8,128)(2,1)S(1)} collective-permute-done((bf16[4,3,176,512]{3,2,1,0:T(8,128)(2,1)S(1)}, bf16[4,3,176,512]{3,2,1,0:T(8,128)(2,1)S(1)}, u32[]{:S(2)}, u32[]{:S(2)}) %collective-permute-start.21) | collective-permute-done | bytes 2162720 | tf_op jit(solution)/shard_map/ppermute | solution.py:571
  215.2 2.4 out_grads.1
  219.5 3.5 all-to-all-start.1
  226.0 2.7 collective-permute-start.20
  230.9 4.9 %collective-permute-done.24 = bf16[4,64,512]{2,1,0:T(8,128)(2,1)S(1)} collective-permute-done((bf16[4,64,512]{2,1,0:T(8,128)(2,1)S(1)}, bf16[4,64,512]{2,1,0:T(8,128)(2,1)S(1)}, u32[]{:S(2)}, u32[]{:S(2)}) %collective-permute-start.24) | collective-permute-done | bytes 262176 | tf_op jit(solution)/shard_map/ppermute | solution.py:571
  236.1 19.2 %all-to-all-done.1 = bf16[288,4,256]{2,0,1:T(8,128)(2,1)S(1)} async-done(((bf16[288,4,256]{2,0,1:T(8,128)(2,1)}), bf16[288,4,256]{2,0,1:T(8,128)(2,1)S(1)}, u32[]{:S(2)}, u32[]{:S(2)}) %all-to-all-start.1) | async-done | bytes 589856 | tf_op jit(solution)/shard_map/all_to_all | solution.py:726
  258.3 9.0 %attn_bwd.1 = (bf16[1152,768]{1,0:T(8,128)(2,1)S(1)}, f32[4,3,128,128]{3,2,1,0:T(8,128)S(1)}, f32[4,2,8,128]{3,2,1,0:T(8,128)S(1)}) custom-call(s32[1,1152]{1,0:T(1,128)S(1)} %copy-done.35, f32[32,4]{1,0:T(8,128)S(1)} %copy-done.29, bf16[1152,768]{1,0:T(8,128)(2,1)} %copy-done.4, bf16[1152,256]{1,0:T(8,128)(2,1)S(1)} %copy-done.19, ...), custom_call_target="tpu_custom_call" | custom-call | flops 1000 | bytes 1000 | tf_op jit(solution)/shard_map/attn_bwd/pallas_call | solution.py:256
  273.0 3.5 normed_grad.1
  280.7 4.0 %qkv_grads.1 = (bf16[4,128,768]{2,1,0:T(8,128)(2,1)S(1)}, bf16[4,128,768]{2,1,0:T(8,128)(2,1)}, f32[8,128]{1,0:T(8,128)S(1)}) custom-call(s32[4]{0:T(128)S(1)} %copy-done.32, bf16[1152,1024]{1,0:T(8,128)(2,1)S(1)} %fusion.33.x_ref, bf16[1152,768]{1,0:T(8,128)(2,1)S(1)} %copy-done.12, bf16[1024,768]{1,0:T(8,128)(2,1)S(1)} %copy-done.9), custom_call_target="tpu_custom_call" | custom-call | flops 1000 | bytes 1000 | tf_op jit(solution)/shard_map/qkv_grads/pallas_call | solution.py:475
  284.7 9.0 %collective-permute-start.25 = (bf16[4,128,768]{2,1,0:T(8,128)(2,1)}, bf16[4,128,768]{2,1,0:T(8,128)(2,1)S(1)}, u32[]{:S(2)}, u32[]{:S(2)}) collective-permute-start(bf16[4,128,768]{2,1,0:T(8,128)(2,1)} %get-tuple-element.123), channel_id=1, source_target_pairs={{0,4},{4,0},{8,12},{12,8},{16,20},{20,16},{24,28},{28,24},{1,5},{5... | collective-permute-start | bytes 2359304 | tf_op jit(solution)/shard_map/ppermute | solution.py:571
  298.9 5.5 %collective-permute-done.31 = bf16[64,512]{1,0:T(8,128)(2,1)S(1)} collective-permute-done((bf16[64,512]{1,0:T(8,128)(2,1)S(1)}, bf16[64,512]{1,0:T(8,128)(2,1)S(1)}, u32[]{:S(2)}, u32[]{:S(2)}) %collective-permute-start.31) | collective-permute-done | bytes 65568 | tf_op jit(solution)/shard_map/ppermute | solution.py:576
  304.8 5.4 %collective-permute-done.30 = bf16[64,512]{1,0:T(8,128)(2,1)S(1)} collective-permute-done((bf16[64,512]{1,0:T(8,128)(2,1)S(1)}, bf16[64,512]{1,0:T(8,128)(2,1)S(1)}, u32[]{:S(2)}, u32[]{:S(2)}) %collective-permute-start.30) | collective-permute-done | bytes 65568 | tf_op jit(solution)/shard_map/ppermute | solution.py:576
  310.2 2.5 collective-permute-start.28
  314.6 7.0 %collective-permute-done.33 = bf16[528,512]{1,0:T(8,128)(2,1)S(1)} collective-permute-done((bf16[528,512]{1,0:T(8,128)(2,1)}, bf16[528,512]{1,0:T(8,128)(2,1)S(1)}, u32[]{:S(2)}, u32[]{:S(2)}) %collective-permute-start.33) | collective-permute-done | bytes 540704 | tf_op jit(solution)/shard_map/ppermute | solution.py:571
  322.0 3.8 collective-permute-done.28
  325.8 3.2 collective-permute-done.27
  332.7 3.4 multiply_reduce_fusion.1
  336.1 2.0 fusion.44
  338.1 3.6 bias_grad.1
  342.5 3.1 collective-permute-done.36
  345.6 2.3 pad_maximum_fusion.1.own_ref
  348.8 3.1 collective-permute-done.40
  352.5 3.3 collective-permute-done.41
  359.5 2.5 collective-permute-done.43
  364.6 3.9 %place_late.1 = (f32[1024,256]{1,0:T(8,128)}, f32[1024,256]{1,0:T(8,128)}, f32[1024,256]{1,0:T(8,128)}, f32[256,1024]{1,0:T(8,128)}) custom-call(s32[4]{0:T(128)} %pad_add_fusion.where_ref, bf16[4,192,768]{2,1,0:T(8,128)(2,1)} %pad_maximum_fusion.1.own_ref, bf16[4,192,768]{2,1,0:T(8,128)(2,1)} %collective-permute-done.38.other_ref), custom_call_target="tpu_custom_call" | custom-call | flops 1000 | bytes 1000 | tf_op jit(solution)/shard_map/place_late/pallas_call | solution.py:535
  368.5 5.6 %place.1 = (f32[704,1024]{1,0:T(8,128)}, f32[704,1024]{1,0:T(8,128)}, f32[704,1024]{1,0:T(8,128)}) custom-call(s32[4]{0:T(128)S(1)} %copy-done.33, bf16[4,528,512]{2,1,0:T(8,128)(2,1)S(1)} %pad_maximum_fusion.own_ref, bf16[4,528,512]{2,1,0:T(8,128)(2,1)} %collective-permute-done.45.other_ref), custom_call_target="tpu_custom_call" | custom-call | flops 1000 | bytes 1000 | tf_op jit(solution)/shard_map/place/pallas_call | solution.py:503
  (271 shorter events, 87.1 us)
Async XLA Ops:
  7.2 125.2 %all-gather.3.cloned.1.call-start = ((), (), s32[]{:S(2)}) async-start(), calls=%async_computation.6 | async-start | bytes 2703360 | tf_op jit(solution)/shard_map/all_gather | solution.py:673
  10.2 20.1 %collective-permute-start = (bf16[320,1024]{1,0:T(8,128)(2,1)}, bf16[320,1024]{1,0:T(8,128)(2,1)}, u32[]{:S(2)}, u32[]{:S(2)}) collective-permute-start(bf16[320,1024]{1,0:T(8,128)(2,1)} %pad_maximum_fusion.3), channel_id=1, source_target_pairs={{0,1},{1,2},{2,3},{3,0},{4,5},{5,6},{6,7},{7,4},{8,9},{9,10},{10,1... | collective-permute-start | bytes 1966088 | tf_op jit(solution)/shard_map/ppermute | solution.py:576
  30.3 43.9 %collective-permute-start.3 = (bf16[288,1024]{1,0:T(8,128)(2,1)S(1)}, bf16[288,1024]{1,0:T(8,128)(2,1)S(1)}, u32[]{:S(2)}, u32[]{:S(2)}) collective-permute-start(bf16[288,1024]{1,0:T(8,128)(2,1)S(1)} %bitcast.123), channel_id=1, source_target_pairs={{0,8},{4,12},{8,0},{12,4},{16,24},{20,28},{24,16},{28,20},{1,9},{5... | collective-permute-start | bytes 1769480 | tf_op jit(solution)/shard_map/ppermute | solution.py:571
  31.8 45.3 %collective-permute-start.4 = (bf16[288,1024]{1,0:T(8,128)(2,1)S(1)}, bf16[288,1024]{1,0:T(8,128)(2,1)}, u32[]{:S(2)}, u32[]{:S(2)}) collective-permute-start(bf16[288,1024]{1,0:T(8,128)(2,1)S(1)} %bitcast.124), channel_id=1, source_target_pairs={{0,16},{4,20},{8,24},{12,28},{16,0},{20,4},{24,8},{28,12},{1,17},{... | collective-permute-start | bytes 1769480 | tf_op jit(solution)/shard_map/ppermute | solution.py:571
  33.3 43.8 %collective-permute-start.5 = (bf16[288,1024]{1,0:T(8,128)(2,1)S(1)}, bf16[288,1024]{1,0:T(8,128)(2,1)}, u32[]{:S(2)}, u32[]{:S(2)}) collective-permute-start(bf16[288,1024]{1,0:T(8,128)(2,1)S(1)} %bitcast.125), channel_id=1, source_target_pairs={{0,24},{4,28},{8,16},{12,20},{16,8},{20,12},{24,0},{28,4},{1,25},{... | collective-permute-start | bytes 1769480 | tf_op jit(solution)/shard_map/ppermute | solution.py:571
  35.1 17.1 %collective-permute-start.1 = (bf16[320,1024]{1,0:T(8,128)(2,1)}, bf16[320,1024]{1,0:T(8,128)(2,1)S(1)}, u32[]{:S(2)}, u32[]{:S(2)}) collective-permute-start(bf16[320,1024]{1,0:T(8,128)(2,1)} %collective-permute-done), channel_id=1, source_target_pairs={{0,1},{1,2},{2,3},{3,0},{4,5},{5,6},{6,7},{7,4},{8,9},{9,10},{10,1... | collective-permute-start | bytes 1966088 | tf_op jit(solution)/shard_map/ppermute | solution.py:576
  52.2 16.3 %collective-permute-start.2 = (bf16[320,1024]{1,0:T(8,128)(2,1)S(1)}, bf16[320,1024]{1,0:T(8,128)(2,1)}, u32[]{:S(2)}, u32[]{:S(2)}) collective-permute-start(bf16[320,1024]{1,0:T(8,128)(2,1)S(1)} %collective-permute-done.1), channel_id=1, source_target_pairs={{0,1},{1,2},{2,3},{3,0},{4,5},{5,6},{6,7},{7,4},{8,9},{9,10},{10,1... | collective-permute-start | bytes 1966088 | tf_op jit(solution)/shard_map/ppermute | solution.py:576
  70.4 14.5 %collective-permute-start.8 = (bf16[4,32,1024]{2,1,0:T(8,128)(2,1)S(1)}, bf16[4,32,1024]{2,1,0:T(8,128)(2,1)S(1)}, u32[]{:S(2)}, u32[]{:S(2)}) collective-permute-start(bf16[4,32,1024]{2,1,0:T(8,128)(2,1)S(1)} %get-tuple-element.184), channel_id=1, source_target_pairs={{0,24},{4,28},{8,16},{12,20},{16,8},{20,12},{24,0},{28,4},{1,25},{... | collective-permute-start | bytes 786440 | tf_op jit(solution)/shard_map/ppermute | solution.py:571
  72.4 12.5 %collective-permute-start.7 = (bf16[4,32,1024]{2,1,0:T(8,128)(2,1)S(1)}, bf16[4,32,1024]{2,1,0:T(8,128)(2,1)S(1)}, u32[]{:S(2)}, u32[]{:S(2)}) collective-permute-start(bf16[4,32,1024]{2,1,0:T(8,128)(2,1)S(1)} %get-tuple-element.184), channel_id=1, source_target_pairs={{0,16},{4,20},{8,24},{12,28},{16,0},{20,4},{24,8},{28,12},{1,17},{... | collective-permute-start | bytes 786440 | tf_op jit(solution)/shard_map/ppermute | solution.py:571
  74.3 10.6 %collective-permute-start.6 = (bf16[4,32,1024]{2,1,0:T(8,128)(2,1)S(1)}, bf16[4,32,1024]{2,1,0:T(8,128)(2,1)S(1)}, u32[]{:S(2)}, u32[]{:S(2)}) collective-permute-start(bf16[4,32,1024]{2,1,0:T(8,128)(2,1)S(1)} %get-tuple-element.184), channel_id=1, source_target_pairs={{0,8},{4,12},{8,0},{12,4},{16,24},{20,28},{24,16},{28,20},{1,9},{5... | collective-permute-start | bytes 786440 | tf_op jit(solution)/shard_map/ppermute | solution.py:571
  86.1 38.9 %collective-permute-start.9 = (bf16[4,4,32,1024]{3,2,1,0:T(8,128)(2,1)}, bf16[4,4,32,1024]{3,2,1,0:T(8,128)(2,1)}, u32[]{:S(2)}, u32[]{:S(2)}) collective-permute-start(bf16[4,4,32,1024]{3,2,1,0:T(8,128)(2,1)} %pad_maximum_fusion.2.mine_ref), channel_id=1, source_target_pairs={{0,4},{4,0},{8,12},{12,8},{16,20},{20,16},{24,28},{28,24},{1,5},{5... | collective-permute-start | bytes 3145736 | tf_op jit(solution)/shard_map/ppermute | solution.py:571
  91.1 33.9 %all-to-all-start = ((bf16[4,288,256]{2,1,0:T(8,128)(2,1)}), bf16[4,288,256]{2,1,0:T(8,128)(2,1)S(1)}, u32[]{:S(2)}, u32[]{:S(2)}) async-start(bf16[4,288,256]{2,1,0:T(8,128)(2,1)} %bitcast.128), calls=%async_computation | async-start | bytes 1179648 | tf_op jit(solution)/shard_map/all_to_all | solution.py:687
  94.5 176.9 %reduce-scatter.3.cloned.1.call-start = ((), (), s32[]{:S(2)}) async-start(), calls=%async_computation.4 | async-start | bytes 2703360 | tf_op jit(solution)/shard_map/reduce_scatter | solution.py:730
  132.5 4.5 %collective-permute-start.10 = (bf16[4,528,512]{2,1,0:T(8,128)(2,1)}, bf16[4,528,512]{2,1,0:T(8,128)(2,1)S(1)}, u32[]{:S(2)}, u32[]{:S(2)}) collective-permute-start(bf16[4,528,512]{2,1,0:T(8,128)(2,1)} %bitcast.118), channel_id=1, source_target_pairs={{0,4},{4,0},{8,12},{12,8},{16,20},{20,16},{24,28},{28,24},{1,5},{5... | collective-permute-start | bytes 6488072 | tf_op jit(solution)/shard_map/ppermute | solution.py:571
  132.5 16.6 %collective-permute-start.11 = (bf16[288,1024]{1,0:T(8,128)(2,1)S(1)}, bf16[288,1024]{1,0:T(8,128)(2,1)S(1)}, u32[]{:S(2)}, u32[]{:S(2)}) collective-permute-start(bf16[288,1024]{1,0:T(8,128)(2,1)S(1)} %multiply_convert_fusion.x_ref.refs_12_), channel_id=1, source_target_pairs={{0,8},{4,12},{8,0},{12,4},{16,24},{20,28},{24,16},{28,20},{1,9},{5... | collective-permute-start | bytes 1769480 | tf_op jit(solution)/shard_map/ppermute | solution.py:571
  135.0 28.0 %collective-permute-start.12 = (bf16[288,1024]{1,0:T(8,128)(2,1)S(1)}, bf16[288,1024]{1,0:T(8,128)(2,1)S(1)}, u32[]{:S(2)}, u32[]{:S(2)}) collective-permute-start(bf16[288,1024]{1,0:T(8,128)(2,1)S(1)} %multiply_convert_fusion.x_ref.refs_12_), channel_id=1, source_target_pairs={{0,16},{4,20},{8,24},{12,28},{16,0},{20,4},{24,8},{28,12},{1,17},{... | collective-permute-start | bytes 1769480 | tf_op jit(solution)/shard_map/ppermute | solution.py:571
  136.5 33.5 %collective-permute-start.13 = (bf16[288,1024]{1,0:T(8,128)(2,1)S(1)}, bf16[288,1024]{1,0:T(8,128)(2,1)S(1)}, u32[]{:S(2)}, u32[]{:S(2)}) collective-permute-start(bf16[288,1024]{1,0:T(8,128)(2,1)S(1)} %multiply_convert_fusion.x_ref.refs_12_), channel_id=1, source_target_pairs={{0,24},{4,28},{8,16},{12,20},{16,8},{20,12},{24,0},{28,4},{1,25},{... | collective-permute-start | bytes 1769480 | tf_op jit(solution)/shard_map/ppermute | solution.py:571
  177.2 17.2 %collective-permute-start.16 = (bf16[288,1024]{1,0:T(8,128)(2,1)S(1)}, bf16[288,1024]{1,0:T(8,128)(2,1)S(1)}, u32[]{:S(2)}, u32[]{:S(2)}) collective-permute-start(bf16[288,1024]{1,0:T(8,128)(2,1)S(1)} %get-tuple-element.104), channel_id=1, source_target_pairs={{0,24},{4,28},{8,16},{12,20},{16,8},{20,12},{24,0},{28,4},{1,25},{... | collective-permute-start | bytes 1769480 | tf_op jit(solution)/shard_map/ppermute | solution.py:571
  177.3 26.9 %collective-permute-start.15 = (bf16[288,1024]{1,0:T(8,128)(2,1)S(1)}, bf16[288,1024]{1,0:T(8,128)(2,1)S(1)}, u32[]{:S(2)}, u32[]{:S(2)}) collective-permute-start(bf16[288,1024]{1,0:T(8,128)(2,1)S(1)} %get-tuple-element.91), channel_id=1, source_target_pairs={{0,16},{4,20},{8,24},{12,28},{16,0},{20,4},{24,8},{28,12},{1,17},{... | collective-permute-start | bytes 1769480 | tf_op jit(solution)/shard_map/ppermute | solution.py:571
  178.8 26.5 %collective-permute-start.14 = (bf16[288,1024]{1,0:T(8,128)(2,1)S(1)}, bf16[288,1024]{1,0:T(8,128)(2,1)S(1)}, u32[]{:S(2)}, u32[]{:S(2)}) collective-permute-start(bf16[288,1024]{1,0:T(8,128)(2,1)S(1)} %get-tuple-element.88), channel_id=1, source_target_pairs={{0,8},{4,12},{8,0},{12,4},{16,24},{20,28},{24,16},{28,20},{1,9},{5... | collective-permute-start | bytes 1769480 | tf_op jit(solution)/shard_map/ppermute | solution.py:571
  208.9 4.3 %collective-permute-start.21 = (bf16[4,3,176,512]{3,2,1,0:T(8,128)(2,1)S(1)}, bf16[4,3,176,512]{3,2,1,0:T(8,128)(2,1)S(1)}, u32[]{:S(2)}, u32[]{:S(2)}) collective-permute-start(bf16[4,3,176,512]{3,2,1,0:T(8,128)(2,1)S(1)} %copy-done.62), channel_id=1, source_target_pairs={{0,4},{4,0},{8,12},{12,8},{16,20},{20,16},{24,28},{28,24},{1,5},{5... | collective-permute-start | bytes 6488072 | tf_op jit(solution)/shard_map/ppermute | solution.py:571
  218.5 4.8 %collective-permute-start.17 = (bf16[4,4,64,512]{3,2,1,0:T(8,128)(2,1)}, bf16[4,4,64,512]{3,2,1,0:T(8,128)(2,1)}, u32[]{:S(2)}, u32[]{:S(2)}) collective-permute-start(bf16[4,4,64,512]{3,2,1,0:T(8,128)(2,1)} %get-tuple-element.107), channel_id=1, source_target_pairs={{0,4},{4,0},{8,12},{12,8},{16,20},{20,16},{24,28},{28,24},{1,5},{5... | collective-permute-start | bytes 3145736 | tf_op jit(solution)/shard_map/ppermute | solution.py:571
  219.5 35.8 %all-to-all-start.1 = ((bf16[288,4,256]{2,0,1:T(8,128)(2,1)}), bf16[288,4,256]{2,0,1:T(8,128)(2,1)S(1)}, u32[]{:S(2)}, u32[]{:S(2)}) async-start(bf16[288,4,256]{2,0,1:T(8,128)(2,1)} %bitcast.117), calls=%async_computation.1 | async-start | bytes 1179648 | tf_op jit(solution)/shard_map/all_to_all | solution.py:726
  223.0 151.1 %reduce-scatter.5.cloned.1.call-start = ((), (), s32[]{:S(2)}) async-start(), calls=%async_computation.5 | async-start | bytes 2949120 | tf_op jit(solution)/shard_map/reduce_scatter | solution.py:748
  225.7 10.2 %collective-permute-start.24 = (bf16[4,64,512]{2,1,0:T(8,128)(2,1)S(1)}, bf16[4,64,512]{2,1,0:T(8,128)(2,1)S(1)}, u32[]{:S(2)}, u32[]{:S(2)}) collective-permute-start(bf16[4,64,512]{2,1,0:T(8,128)(2,1)S(1)} %get-tuple-element.175), channel_id=1, source_target_pairs={{0,24},{4,28},{8,16},{12,20},{16,8},{20,12},{24,0},{28,4},{1,25},{... | collective-permute-start | bytes 786440 | tf_op jit(solution)/shard_map/ppermute | solution.py:571
  226.0 45.4 %collective-permute-start.20 = (bf16[288,1024]{1,0:T(8,128)(2,1)}, bf16[288,1024]{1,0:T(8,128)(2,1)}, u32[]{:S(2)}, u32[]{:S(2)}) collective-permute-start(bf16[288,1024]{1,0:T(8,128)(2,1)} %get-tuple-element.114), channel_id=1, source_target_pairs={{0,24},{4,28},{8,16},{12,20},{16,8},{20,12},{24,0},{28,4},{1,25},{... | collective-permute-start | bytes 1769480 | tf_op jit(solution)/shard_map/ppermute | solution.py:571
  228.7 42.8 %collective-permute-start.19 = (bf16[288,1024]{1,0:T(8,128)(2,1)}, bf16[288,1024]{1,0:T(8,128)(2,1)}, u32[]{:S(2)}, u32[]{:S(2)}) collective-permute-start(bf16[288,1024]{1,0:T(8,128)(2,1)} %get-tuple-element.112), channel_id=1, source_target_pairs={{0,16},{4,20},{8,24},{12,28},{16,0},{20,4},{24,8},{28,12},{1,17},{... | collective-permute-start | bytes 1769480 | tf_op jit(solution)/shard_map/ppermute | solution.py:571
  229.3 42.2 %collective-permute-start.18 = (bf16[288,1024]{1,0:T(8,128)(2,1)}, bf16[288,1024]{1,0:T(8,128)(2,1)}, u32[]{:S(2)}, u32[]{:S(2)}) collective-permute-start(bf16[288,1024]{1,0:T(8,128)(2,1)} %get-tuple-element.110), channel_id=1, source_target_pairs={{0,8},{4,12},{8,0},{12,4},{16,24},{20,28},{24,16},{28,20},{1,9},{5... | collective-permute-start | bytes 1769480 | tf_op jit(solution)/shard_map/ppermute | solution.py:571
  229.5 39.9 %collective-permute-start.23 = (bf16[4,64,512]{2,1,0:T(8,128)(2,1)}, bf16[4,64,512]{2,1,0:T(8,128)(2,1)S(1)}, u32[]{:S(2)}, u32[]{:S(2)}) collective-permute-start(bf16[4,64,512]{2,1,0:T(8,128)(2,1)} %get-tuple-element.176), channel_id=1, source_target_pairs={{0,16},{4,20},{8,24},{12,28},{16,0},{20,4},{24,8},{28,12},{1,17},{... | collective-permute-start | bytes 786440 | tf_op jit(solution)/shard_map/ppermute | solution.py:571
  235.9 34.3 %collective-permute-start.22 = (bf16[4,64,512]{2,1,0:T(8,128)(2,1)}, bf16[4,64,512]{2,1,0:T(8,128)(2,1)}, u32[]{:S(2)}, u32[]{:S(2)}) collective-permute-start(bf16[4,64,512]{2,1,0:T(8,128)(2,1)} %get-tuple-element.174), channel_id=1, source_target_pairs={{0,8},{4,12},{8,0},{12,4},{16,24},{20,28},{24,16},{28,20},{1,9},{5... | collective-permute-start | bytes 786440 | tf_op jit(solution)/shard_map/ppermute | solution.py:571
  284.7 14.0 %collective-permute-start.25 = (bf16[4,128,768]{2,1,0:T(8,128)(2,1)}, bf16[4,128,768]{2,1,0:T(8,128)(2,1)S(1)}, u32[]{:S(2)}, u32[]{:S(2)}) collective-permute-start(bf16[4,128,768]{2,1,0:T(8,128)(2,1)} %get-tuple-element.123), channel_id=1, source_target_pairs={{0,4},{4,0},{8,12},{12,8},{16,20},{20,16},{24,28},{28,24},{1,5},{5... | collective-permute-start | bytes 2359304 | tf_op jit(solution)/shard_map/ppermute | solution.py:571
  293.7 19.5 %collective-permute-start.34 = (bf16[528,512]{1,0:T(8,128)(2,1)}, bf16[528,512]{1,0:T(8,128)(2,1)S(1)}, u32[]{:S(2)}, u32[]{:S(2)}) collective-permute-start(bf16[528,512]{1,0:T(8,128)(2,1)} %bitcast.136), channel_id=1, source_target_pairs={{0,24},{4,28},{8,16},{12,20},{16,8},{20,12},{24,0},{28,4},{1,25},{... | collective-permute-start | bytes 1622024 | tf_op jit(solution)/shard_map/ppermute | solution.py:571
  295.7 25.9 %collective-permute-start.33 = (bf16[528,512]{1,0:T(8,128)(2,1)}, bf16[528,512]{1,0:T(8,128)(2,1)S(1)}, u32[]{:S(2)}, u32[]{:S(2)}) collective-permute-start(bf16[528,512]{1,0:T(8,128)(2,1)} %bitcast.137), channel_id=1, source_target_pairs={{0,16},{4,20},{8,24},{12,28},{16,0},{20,4},{24,8},{28,12},{1,17},{... | collective-permute-start | bytes 1622024 | tf_op jit(solution)/shard_map/ppermute | solution.py:571
  296.5 25.2 %collective-permute-start.32 = (bf16[528,512]{1,0:T(8,128)(2,1)}, bf16[528,512]{1,0:T(8,128)(2,1)S(1)}, u32[]{:S(2)}, u32[]{:S(2)}) collective-permute-start(bf16[528,512]{1,0:T(8,128)(2,1)} %bitcast.138), channel_id=1, source_target_pairs={{0,8},{4,12},{8,0},{12,4},{16,24},{20,28},{24,16},{28,20},{1,9},{5... | collective-permute-start | bytes 1622024 | tf_op jit(solution)/shard_map/ppermute | solution.py:571
  297.2 7.2 %collective-permute-start.31 = (bf16[64,512]{1,0:T(8,128)(2,1)S(1)}, bf16[64,512]{1,0:T(8,128)(2,1)S(1)}, u32[]{:S(2)}, u32[]{:S(2)}) collective-permute-start(bf16[64,512]{1,0:T(8,128)(2,1)S(1)} %get-tuple-element.181), channel_id=1, source_target_pairs={{0,3},{1,0},{2,1},{3,2},{4,7},{5,4},{6,5},{7,6},{8,11},{9,8},{10,9... | collective-permute-start | bytes 196616 | tf_op jit(solution)/shard_map/ppermute | solution.py:576
  298.7 11.4 %collective-permute-start.30 = (bf16[64,512]{1,0:T(8,128)(2,1)S(1)}, bf16[64,512]{1,0:T(8,128)(2,1)S(1)}, u32[]{:S(2)}, u32[]{:S(2)}) collective-permute-start(bf16[64,512]{1,0:T(8,128)(2,1)S(1)} %get-tuple-element.182), channel_id=1, source_target_pairs={{0,2},{1,3},{2,0},{3,1},{4,6},{5,7},{6,4},{7,5},{8,10},{9,11},{10,... | collective-permute-start | bytes 196616 | tf_op jit(solution)/shard_map/ppermute | solution.py:576
  304.5 8.2 %collective-permute-start.29 = (bf16[64,512]{1,0:T(8,128)(2,1)S(1)}, bf16[64,512]{1,0:T(8,128)(2,1)S(1)}, u32[]{:S(2)}, u32[]{:S(2)}) collective-permute-start(bf16[64,512]{1,0:T(8,128)(2,1)S(1)} %get-tuple-element.180), channel_id=1, source_target_pairs={{0,1},{1,2},{2,3},{3,0},{4,5},{5,6},{6,7},{7,4},{8,9},{9,10},{10,1... | collective-permute-start | bytes 196616 | tf_op jit(solution)/shard_map/ppermute | solution.py:576
  310.2 15.7 %collective-permute-start.28 = (bf16[128,768]{1,0:T(8,128)(2,1)S(1)}, bf16[128,768]{1,0:T(8,128)(2,1)S(1)}, u32[]{:S(2)}, u32[]{:S(2)}) collective-permute-start(bf16[128,768]{1,0:T(8,128)(2,1)S(1)} %get-tuple-element.178), channel_id=1, source_target_pairs={{0,24},{4,28},{8,16},{12,20},{16,8},{20,12},{24,0},{28,4},{1,25},{... | collective-permute-start | bytes 589832 | tf_op jit(solution)/shard_map/ppermute | solution.py:571
  312.7 16.3 %collective-permute-start.27 = (bf16[128,768]{1,0:T(8,128)(2,1)S(1)}, bf16[128,768]{1,0:T(8,128)(2,1)S(1)}, u32[]{:S(2)}, u32[]{:S(2)}) collective-permute-start(bf16[128,768]{1,0:T(8,128)(2,1)S(1)} %get-tuple-element.179), channel_id=1, source_target_pairs={{0,16},{4,20},{8,24},{12,28},{16,0},{20,4},{24,8},{28,12},{1,17},{... | collective-permute-start | bytes 589832 | tf_op jit(solution)/shard_map/ppermute | solution.py:571
  313.3 15.8 %collective-permute-start.26 = (bf16[128,768]{1,0:T(8,128)(2,1)S(1)}, bf16[128,768]{1,0:T(8,128)(2,1)S(1)}, u32[]{:S(2)}, u32[]{:S(2)}) collective-permute-start(bf16[128,768]{1,0:T(8,128)(2,1)S(1)} %get-tuple-element.177), channel_id=1, source_target_pairs={{0,8},{4,12},{8,0},{12,4},{16,24},{20,28},{24,16},{28,20},{1,9},{5... | collective-permute-start | bytes 589832 | tf_op jit(solution)/shard_map/ppermute | solution.py:571
  321.9 46.6 %collective-permute-start.45 = (bf16[4,528,512]{2,1,0:T(8,128)(2,1)S(1)}, bf16[4,528,512]{2,1,0:T(8,128)(2,1)}, u32[]{:S(2)}, u32[]{:S(2)}) collective-permute-start(bf16[4,528,512]{2,1,0:T(8,128)(2,1)S(1)} %pad_maximum_fusion.own_ref), channel_id=1, source_target_pairs={{0,4},{4,0},{8,12},{12,8},{16,20},{20,16},{24,28},{28,24},{1,5},{5... | collective-permute-start | bytes 6488072 | tf_op jit(solution)/shard_map/ppermute | solution.py:571
  329.2 13.3 %collective-permute-start.37 = (bf16[192,768]{1,0:T(8,128)(2,1)S(1)}, bf16[192,768]{1,0:T(8,128)(2,1)}, u32[]{:S(2)}, u32[]{:S(2)}) collective-permute-start(bf16[192,768]{1,0:T(8,128)(2,1)S(1)} %fusion.27), channel_id=1, source_target_pairs={{0,24},{4,28},{8,16},{12,20},{16,8},{20,12},{24,0},{28,4},{1,25},{... | collective-permute-start | bytes 884744 | tf_op jit(solution)/shard_map/ppermute | solution.py:571
  331.0 14.6 %collective-permute-start.36 = (bf16[192,768]{1,0:T(8,128)(2,1)S(1)}, bf16[192,768]{1,0:T(8,128)(2,1)}, u32[]{:S(2)}, u32[]{:S(2)}) collective-permute-start(bf16[192,768]{1,0:T(8,128)(2,1)S(1)} %fusion.27), channel_id=1, source_target_pairs={{0,16},{4,20},{8,24},{12,28},{16,0},{20,4},{24,8},{28,12},{1,17},{... | collective-permute-start | bytes 884744 | tf_op jit(solution)/shard_map/ppermute | solution.py:571
  332.4 13.2 %collective-permute-start.35 = (bf16[192,768]{1,0:T(8,128)(2,1)S(1)}, bf16[192,768]{1,0:T(8,128)(2,1)}, u32[]{:S(2)}, u32[]{:S(2)}) collective-permute-start(bf16[192,768]{1,0:T(8,128)(2,1)S(1)} %fusion.27), channel_id=1, source_target_pairs={{0,8},{4,12},{8,0},{12,4},{16,24},{20,28},{24,16},{28,20},{1,9},{5... | collective-permute-start | bytes 884744 | tf_op jit(solution)/shard_map/ppermute | solution.py:571
  342.5 5.5 %collective-permute-start.39 = (f32[49,128]{1,0:T(8,128)S(1)}, f32[49,128]{1,0:T(8,128)S(1)}, u32[]{:S(2)}, u32[]{:S(2)}) collective-permute-start(f32[49,128]{1,0:T(8,128)S(1)} %pad_maximum_fusion.6), channel_id=1, source_target_pairs={{0,4},{4,0},{8,12},{12,8},{16,20},{20,16},{24,28},{28,24},{1,5},{5... | collective-permute-start | bytes 75272 | tf_op jit(solution)/shard_map/ppermute | solution.py:571
  347.9 16.7 %collective-permute-start.38 = (bf16[4,192,768]{2,1,0:T(8,128)(2,1)}, bf16[4,192,768]{2,1,0:T(8,128)(2,1)}, u32[]{:S(2)}, u32[]{:S(2)}) collective-permute-start(bf16[4,192,768]{2,1,0:T(8,128)(2,1)} %pad_maximum_fusion.1.own_ref), channel_id=1, source_target_pairs={{0,4},{4,0},{8,12},{12,8},{16,20},{20,16},{24,28},{28,24},{1,5},{5... | collective-permute-start | bytes 3538952 | tf_op jit(solution)/shard_map/ppermute | solution.py:571
  357.4 4.6 %collective-permute-start.43 = (f32[17,128]{1,0:T(8,128)S(1)}, f32[17,128]{1,0:T(8,128)S(1)}, u32[]{:S(2)}, u32[]{:S(2)}) collective-permute-start(f32[17,128]{1,0:T(8,128)S(1)} %slice.90), channel_id=1, source_target_pairs={{0,2},{1,3},{2,0},{3,1},{4,6},{5,7},{6,4},{7,5},{8,10},{9,11},{10,... | collective-permute-start | bytes 26120 | tf_op jit(solution)/shard_map/ppermute | solution.py:576
  357.4 5.5 %collective-permute-start.42 = (f32[17,128]{1,0:T(8,128)S(1)}, f32[17,128]{1,0:T(8,128)S(1)}, u32[]{:S(2)}, u32[]{:S(2)}) collective-permute-start(f32[17,128]{1,0:T(8,128)S(1)} %slice.90), channel_id=1, source_target_pairs={{0,1},{1,2},{2,3},{3,0},{4,5},{5,6},{6,7},{7,4},{8,9},{9,10},{10,1... | collective-permute-start | bytes 26120 | tf_op jit(solution)/shard_map/ppermute | solution.py:576
  (67 other events, 678.8 us)
Sparse Core Ops, SparseCore 0:
  68.6 57.3 all-gather.2
  215.3 51.2 reduce-scatter.2
  276.6 60.1 reduce-scatter.4
